TPU v7x, 256 devices: a whole 4x4x8 slice. The times are simulated.
256 devices in a mesh: strip: 4 (over y_lo, core), depth: 64 (over y_hi, x, z).
Axes of the slice: x: 4, y: 4 (y_hi: 2, y_lo: 2; y = y_hi * 2 + y_lo), z: 8, core: 2. Of those that a mesh axis runs over, the one named last changes fastest.
Arguments:
- position: float32 [4, 64, 3, 32, 128], P('strip', 'depth'), may hold values from -2.4 to 2.4
- velocity: float32 [4, 64, 3, 32, 128], P('strip', 'depth'), may hold values from -3 to 3
- stress: float32 [4, 64, 6, 32, 128], P('strip', 'depth'), may hold values from -6 to 6
- plastic: float32 [4, 64, 32, 128], P('strip', 'depth'), may hold values from 0.005 to 0.2
- particle_mass: float32 [4, 64, 32, 128], P('strip', 'depth'), may hold values from 0.004 to 0.016
- density: float32 [4, 64, 32, 128], P('strip', 'depth'), may hold values from 0.6 to 1.6
- cohesion: float32 [4, 64, 32, 128], P('strip', 'depth'), may hold values from 0.3 to 1.2
- counts: int32 [4, 64, 32], P('strip', 'depth'), may hold values from 32 to 128, as said below
- block_pairs: int32 [4, 64, 128, 2], P('strip', 'depth'), may hold values from 0 to 31, as said below
- pair_count: int32 [4, 64], P('strip', 'depth'), may hold values from 32 to 128, as said below
- send_lists: int32 [4, 64, 4, 16], P('strip', 'depth'), may hold values from 0 to 31, as said below
- cross_links: int32 [4, 64, 2, 48, 2], P('strip', 'depth'), may hold values from 0 to 15, as said below
- contact: int32 [4, 64, 16], P('strip', 'depth'), may hold values from 0 to 32, as said below
Outputs:
- new_position: float32 [4, 64, 3, 32, 128], P('strip', 'depth')
- new_velocity: float32 [4, 64, 3, 32, 128], P('strip', 'depth')
- new_stress: float32 [4, 64, 6, 32, 128], P('strip', 'depth')
- new_plastic: float32 [4, 64, 32, 128], P('strip', 'depth')
Inputs may be any that keep to these rules, and one draw needn't show every extreme that they name: A block's live particles are its first counts slots; every device has a full block. `pair_count`: at least 32; some device reaches 128. `block_pairs`: the first pair_count entries of a device hold each of its blocks paired with itself once and distinct unordered pairs of different blocks, each at most once, in either order; later entries are to be ignored. `send_lists`: each face lists 16 distinct blocks; faces 0, 1 look to the next and previous device along depth, 2, 3 along strip. `cross_links`: entry (f, q) = (a, b): slot a of the device's list 2f meets slot b of the next device's list 2f + 1; a face's entries are distinct. `contact`: 32 stands for no block; a device's entries are either all 32 or 16 distinct blocks.
All inputs are finite; a program needn't handle non-finite values.
Results may differ from a plain program's by a relative error of at most 0.0003.
Values sent between devices are 32-bit elements; how exact they have to be, the bound alone decides.
No kernel may reach another device: no remote copies, remote signals or barrier semaphores. Data moves between devices by JAX's collectives and lax.ppermute only.
A program may use at most 64 MiB of HBM per device.

v0:
```python
import jax
import jax.numpy as jnp
from jax import lax
from jax.sharding import PartitionSpec as P

RETURN_ITERS = 4


smooth_len = 1.5
kernel_coef = -105.0 / (3.141592653589793 * 1.5**5)
time_step = 0.25
gravity = 1.0
spin_rate = 2.0
blade_stiff = 4.0
bulk_mod = 2.0
shear_mod = 1.5
friction = 0.25
harden_scale = 0.05
harden_mod = 0.5
relax_rate = 0.7
tau_floor = 0.5
group_tiles = 32
voigt_index = ((0, 3, 5), (3, 1, 4), (5, 4, 2))
voigt_pairs = ((0, 0), (1, 1), (2, 2), (0, 1), (1, 2), (0, 2))


def from_behind(block, axis, distance):
    devices = range(lax.axis_size(axis))
    route = [(i - distance, i) for i in devices if i - distance in devices]
    return lax.ppermute(block, axis, route)


def passed_along(value, axis, steps):
    count = lax.axis_size(axis)
    pairs = [(source, (source + steps) % count) for source in range(count)]
    return lax.ppermute(value, axis, pairs)


def source_rows(places, motion, stress, particle_mass, density, occupied):
    safe_density = jnp.where(occupied > 0.0, density, 1.0)
    weighted_mass = particle_mass * occupied
    volume = weighted_mass / safe_density
    scaled = stress / (safe_density * safe_density)[..., None, :]
    feature_rows = [weighted_mass]
    for row_axis in range(3):
        feature_rows.append(weighted_mass * places[..., row_axis, :])
    for component in range(6):
        feature_rows.append(weighted_mass * scaled[..., component, :])
    for row_axis in range(3):
        dotted = scaled[..., voigt_index[row_axis][0], :] * places[..., 0, :]
        dotted = dotted + scaled[..., voigt_index[row_axis][1], :] * places[..., 1, :]
        dotted = dotted + scaled[..., voigt_index[row_axis][2], :] * places[..., 2, :]
        feature_rows.append(weighted_mass * dotted)
    feature_rows.append(volume)
    for row_axis in range(3):
        feature_rows.append(volume * motion[..., row_axis, :])
    for row_axis in range(3):
        feature_rows.append(volume * places[..., row_axis, :])
    for row_axis, col_axis in voigt_pairs:
        paired = (
            motion[..., row_axis, :] * places[..., col_axis, :]
            + motion[..., col_axis, :] * places[..., row_axis, :]
        )
        feature_rows.append(volume * (0.5 * paired))
    return jnp.stack(feature_rows, axis=-2)


def pair_kernel(row_places, col_places, weight):
    squared = jnp.zeros(
        row_places.shape[:-2] + (row_places.shape[-1], col_places.shape[-1]), jnp.float32
    )
    for row_axis in range(3):
        spread = row_places[..., row_axis, :, None] - col_places[..., row_axis, None, :]
        squared = squared + spread * spread
    closeness = jnp.maximum(1.0 - jnp.sqrt(squared) / smooth_len, 0.0)
    return kernel_coef * closeness * closeness * closeness * weight[..., None, None]


def tile_sums(row_sources, row_places, col_sources, col_places, links_in, tile_total, halve_self):
    length = links_in.shape[0]
    padded = -(-length // group_tiles) * group_tiles
    links_padded = jnp.pad(links_in, ((0, padded - length), (0, 0)))
    offsets = jnp.arange(group_tiles, dtype=jnp.int32)

    def one_group(group_index, carried):
        row_summed, col_summed = carried
        portion = lax.dynamic_slice_in_dim(links_padded, group_index * group_tiles, group_tiles, 0)
        row_block = portion[:, 0]
        col_block = portion[:, 1]
        weight = jnp.where(group_index * group_tiles + offsets < tile_total, 1.0, 0.0).astype(
            jnp.float32
        )
        if halve_self:
            weight = weight * jnp.where(row_block == col_block, 0.5, 1.0)
        kernel = pair_kernel(row_places[row_block], col_places[col_block], weight)
        to_rows = jnp.einsum(
            "tkj,tij->tki", col_sources[col_block], kernel, precision=lax.Precision.HIGHEST
        )
        row_summed = row_summed.at[row_block].add(to_rows)
        to_cols = jnp.einsum(
            "tki,tij->tkj", row_sources[row_block], kernel, precision=lax.Precision.HIGHEST
        )
        col_summed = col_summed.at[col_block].add(to_cols)
        return (row_summed, col_summed)

    groups = (tile_total + group_tiles - 1) // group_tiles
    start_sums = (
        jnp.zeros(row_sources.shape, jnp.float32),
        jnp.zeros(col_sources.shape, jnp.float32),
    )
    return lax.fori_loop(0, groups, one_group, start_sums)


def section_rates(summed, places, motion, stress, density, contact_flag):
    scaled = stress / (density * density)[..., None, :]
    blade_motion = (
        spin_rate * places[..., 2, :],
        jnp.zeros_like(places[..., 1, :]),
        -spin_rate * places[..., 0, :],
    )
    acceleration = []
    for row_axis in range(3):
        total_force = jnp.zeros_like(summed[..., 0, :])
        for col_axis in range(3):
            voigt_slot = voigt_index[row_axis][col_axis]
            total_force = total_force + scaled[..., voigt_slot, :] * (
                places[..., col_axis, :] * summed[..., 0, :] - summed[..., 1 + col_axis, :]
            )
            total_force = total_force + places[..., col_axis, :] * summed[..., 4 + voigt_slot, :]
        total_force = total_force - summed[..., 10 + row_axis, :]
        total_force = total_force + blade_stiff * contact_flag * (
            blade_motion[row_axis] - motion[..., row_axis, :]
        )
        if row_axis == 2:
            total_force = total_force - gravity
        acceleration.append(total_force)
    strain = []
    for component, (row_axis, col_axis) in enumerate(voigt_pairs):
        strain_rate = 0.5 * (
            places[..., col_axis, :] * summed[..., 14 + row_axis, :]
            + places[..., row_axis, :] * summed[..., 14 + col_axis, :]
        )
        strain_rate = strain_rate - summed[..., 20 + component, :]
        strain_rate = strain_rate - 0.5 * summed[..., 13, :] * (
            motion[..., row_axis, :] * places[..., col_axis, :]
            + motion[..., col_axis, :] * places[..., row_axis, :]
        )
        strain_rate = strain_rate + 0.5 * (
            motion[..., row_axis, :] * summed[..., 17 + col_axis, :]
            + motion[..., col_axis, :] * summed[..., 17 + row_axis, :]
        )
        strain.append(strain_rate)
    return (jnp.stack(acceleration, axis=-2), jnp.stack(strain, axis=-2))


def elastic_step(stress, strain, fraction):
    volumetric = strain[..., 0, :] + strain[..., 1, :] + strain[..., 2, :]
    lame_first = bulk_mod - 2.0 * shear_mod / 3.0
    components = []
    for component in range(6):
        change = 2.0 * shear_mod * strain[..., component, :]
        if component < 3:
            change = change + lame_first * volumetric
        components.append(stress[..., component, :] + fraction * time_step * change)
    return components


def plastic_return(components, plastic, cohesion):
    for iteration in range(RETURN_ITERS):
        mean_stress = (components[0] + components[1] + components[2]) / 3.0
        deviator = [
            components[0] - mean_stress,
            components[1] - mean_stress,
            components[2] - mean_stress,
            components[3],
            components[4],
            components[5],
        ]
        second = 0.5 * (
            deviator[0] * deviator[0] + deviator[1] * deviator[1] + deviator[2] * deviator[2]
        )
        second = (
            second
            + deviator[3] * deviator[3]
            + deviator[4] * deviator[4]
            + deviator[5] * deviator[5]
        )
        shear_norm = jnp.sqrt(second)
        yield_limit = cohesion * (1.0 + plastic / (plastic + harden_scale))
        excess = jnp.maximum(shear_norm + friction * 3.0 * mean_stress - yield_limit, 0.0)
        multiplier = (
            relax_rate * excess / (shear_mod + 9.0 * bulk_mod * friction * friction + harden_mod)
        )
        shrink = jnp.maximum(1.0 - shear_mod * multiplier / jnp.maximum(shear_norm, tau_floor), 0.0)
        mean_stress = mean_stress - 3.0 * bulk_mod * friction * multiplier
        components = [
            deviator[0] * shrink + mean_stress,
            deviator[1] * shrink + mean_stress,
            deviator[2] * shrink + mean_stress,
            deviator[3] * shrink,
            deviator[4] * shrink,
            deviator[5] * shrink,
        ]
        plastic = plastic + multiplier
    return (jnp.stack(components, axis=-2), plastic)


def fetch_depth(values_in, offset):
    return from_behind(values_in, "depth", offset)


def fetch_strip(values_in, offset):
    return passed_along(values_in, "strip", offset)


def hand_back_depth(values_in):
    return from_behind(values_in, "depth", 1)


def hand_back_strip(values_in):
    return passed_along(values_in, "strip", 1)


def shards(
    position,
    velocity,
    stress,
    plastic,
    particle_mass,
    density,
    cohesion,
    counts,
    block_pairs,
    pair_count,
    send_lists,
    cross_links,
    contact,
):
    places = jnp.swapaxes(position[0, 0], 0, 1)
    motion = jnp.swapaxes(velocity[0, 0], 0, 1)
    stress_blocks = jnp.swapaxes(stress[0, 0], 0, 1)
    plastic_now = plastic[0, 0]
    mass_now = particle_mass[0, 0]
    density_now = density[0, 0]
    cohesion_now = cohesion[0, 0]
    pairs_now = block_pairs[0, 0]
    pair_total = pair_count[0, 0]
    rim_lists = send_lists[0, 0]
    links_now = cross_links[0, 0]
    blocks = places.shape[0]
    occupied = (
        jnp.arange(places.shape[-1], dtype=jnp.int32)[None, :] < counts[0, 0][:, None]
    ).astype(jnp.float32)
    contact_flag = jnp.sum(
        (contact[0, 0][:, None] == jnp.arange(blocks, dtype=jnp.int32)[None, :]).astype(
            jnp.float32
        ),
        axis=0,
    )[:, None]

    def interact(cur_places, cur_motion, cur_stress):
        sources = source_rows(cur_places, cur_motion, cur_stress, mass_now, density_now, occupied)
        row_part, col_part = tile_sums(
            sources, cur_places, sources, cur_places, pairs_now, pair_total, True
        )
        summed = row_part + col_part
        for face_index in range(2):
            up_rim = rim_lists[2 * face_index]
            down_rim = rim_lists[2 * face_index + 1]
            face_links = links_now[face_index]
            fetch_rows = fetch_depth if face_index == 0 else fetch_strip
            hand_back = hand_back_depth if face_index == 0 else hand_back_strip
            received = fetch_rows(
                jnp.concatenate([cur_places[down_rim], sources[down_rim]], axis=1), -1
            )
            far_sources = received[:, 3:]
            far_places = received[:, 0:3]
            own_part, far_part = tile_sums(
                sources[up_rim],
                cur_places[up_rim],
                far_sources,
                far_places,
                face_links,
                face_links.shape[0],
                False,
            )
            summed = summed.at[up_rim].add(own_part)
            summed = summed.at[down_rim].add(hand_back(far_part))
        return summed

    summed = interact(places, motion, stress_blocks)
    acceleration, strain = section_rates(
        summed, places, motion, stress_blocks, density_now, contact_flag
    )
    half_motion = motion + 0.5 * time_step * acceleration
    half_places = places + 0.5 * time_step * motion
    half_stress = plastic_return(
        elastic_step(stress_blocks, strain, 0.5), plastic_now, cohesion_now
    )[0]
    summed = interact(half_places, half_motion, half_stress)
    acceleration, strain = section_rates(
        summed, half_places, half_motion, half_stress, density_now, contact_flag
    )
    new_motion = motion + time_step * acceleration
    new_places = places + time_step * half_motion
    new_stress, new_plastic = plastic_return(
        elastic_step(stress_blocks, strain, 1.0), plastic_now, cohesion_now
    )
    particle_keep = occupied[:, None, :]
    new_position = jnp.swapaxes(new_places * particle_keep, 0, 1)[None, None]
    new_velocity = jnp.swapaxes(new_motion * particle_keep, 0, 1)[None, None]
    new_stress_out = jnp.swapaxes(new_stress * particle_keep, 0, 1)[None, None]
    new_plastic_out = (new_plastic * occupied)[None, None]
    return (new_position, new_velocity, new_stress_out, new_plastic_out)


def solution(mesh):
    return jax.shard_map(
        shards,
        mesh=mesh,
        in_specs=(
            P("strip", "depth", None, None, None),
            P("strip", "depth", None, None, None),
            P("strip", "depth", None, None, None),
            P("strip", "depth", None, None),
            P("strip", "depth", None, None),
            P("strip", "depth", None, None),
            P("strip", "depth", None, None),
            P("strip", "depth", None),
            P("strip", "depth", None, None),
            P("strip", "depth"),
            P("strip", "depth", None, None),
            P("strip", "depth", None, None, None),
            P("strip", "depth", None),
        ),
        out_specs=(
            P("strip", "depth", None, None, None),
            P("strip", "depth", None, None, None),
            P("strip", "depth", None, None, None),
            P("strip", "depth", None, None),
        ),
        check_vma=False,
    )
```

profile of v0, /device:TPU:24, one launch (start us, length us, event | category | flops | bytes accessed | tf_op | source)
XLA Modules:
  0.0 364.9 jit_solution(4926993698937946430)
XLA Ops:
  6.9 10.6 %collective-permute-start = (f32[16,29,128]{2,1,0:T(8,128)}, f32[16,29,128]{2,1,0:T(8,128)S(1)}, u32[]{:S(2)}, u32[]{:S(2)}) collective-permute-start(f32[16,29,128]{2,1,0:T(8,128)} %pad_maximum_fusion), channel_id=1, source_target_pairs={{1,0},{2,1},{3,2},{4,3},{5,4},{6,5},{7,6},{8,7},{9,8},{10,9},{11,1... | collective-permute-start | bytes 712712 | tf_op jit(solution)/shard_map/ppermute | solution.py:30
  20.8 71.8 %while.90 = (s32[]{:T(128)}, f32[32,26,128]{2,1,0:T(8,128)S(1)}, f32[32,26,128]{2,1,0:T(8,128)S(1)}, s32[]{:T(128)}, s32[128,2]{0,1:T(2,128)S(1)}, /*index=5*/f3...) while((s32[]{:T(128)}, f32[32,26,128]{2,1,0:T(8,128)S(1)}, ...), condition=%wide.region_3.4_spmd.clone, body=%wide.region_0.3_spmd.clone.sunk | while | flops 343099776 | bytes 6564663 | solution.py:111
  23.4 6.1 %fusion.457 = f32[32,26,128]{2,1,0:T(8,128)S(1)} fusion(f32[32,26,128]{2,1,0:T(8,128)S(1)} %gather_fusion, f32[32]{0:T(128)S(1)} %fusion.454, f32[32,128]{1,0:T(8,128)S(1)} %bitcast.559, f32[32,128]{1,0:T(8,128)S(1)} %bitcast.595, f32[32,128]{1,0:T(8,128)S(1)} %bitcast.557, f32[32,128]{1,0:T(8,128)S(1)} %bitcast.593, f32[32,128]{1,0:T(8,128)S(1)} %bitcast.555, ...), kind=kOutput, calls=%fused_computation.69.clone.1 | convolution fusion | flops 171442176 | bytes 950400 | tf_op jit(solution)/shard_map/while/body/tkj,tij->tki/dot_general | solution.py:96
  31.9 4.9 %fusion.458 = f32[32,26,128]{2,1,0:T(8,128)S(1)} fusion(f32[32,26,128]{2,1,0:T(8,128)S(1)} %gather_fusion.3, f32[32]{0:T(128)S(1)} %fusion.454, f32[32,128]{1,0:T(8,128)S(1)} %bitcast.560, f32[32,128]{1,0:T(8,128)S(1)} %bitcast.596, f32[32,128]{1,0:T(8,128)S(1)} %bitcast.558, f32[32,128]{1,0:T(8,128)S(1)} %bitcast.594, f32[32,128]{1,0:T(8,128)S(1)} %bitcast.556, ...), kind=kOutput, calls=%fused_computation.68.clone.1 | convolution fusion | flops 171442176 | bytes 950400 | tf_op jit(solution)/shard_map/while/body/tki,tij->tkj/dot_general | solution.py:100
  41.4 6.1 %fusion.457 = f32[32,26,128]{2,1,0:T(8,128)S(1)} fusion(f32[32,26,128]{2,1,0:T(8,128)S(1)} %gather_fusion, f32[32]{0:T(128)S(1)} %fusion.454, f32[32,128]{1,0:T(8,128)S(1)} %bitcast.559, f32[32,128]{1,0:T(8,128)S(1)} %bitcast.595, f32[32,128]{1,0:T(8,128)S(1)} %bitcast.557, f32[32,128]{1,0:T(8,128)S(1)} %bitcast.593, f32[32,128]{1,0:T(8,128)S(1)} %bitcast.555, ...), kind=kOutput, calls=%fused_computation.69.clone.1 | convolution fusion | flops 171442176 | bytes 950400 | tf_op jit(solution)/shard_map/while/body/tkj,tij->tki/dot_general | solution.py:96
  49.9 4.9 %fusion.458 = f32[32,26,128]{2,1,0:T(8,128)S(1)} fusion(f32[32,26,128]{2,1,0:T(8,128)S(1)} %gather_fusion.3, f32[32]{0:T(128)S(1)} %fusion.454, f32[32,128]{1,0:T(8,128)S(1)} %bitcast.560, f32[32,128]{1,0:T(8,128)S(1)} %bitcast.596, f32[32,128]{1,0:T(8,128)S(1)} %bitcast.558, f32[32,128]{1,0:T(8,128)S(1)} %bitcast.594, f32[32,128]{1,0:T(8,128)S(1)} %bitcast.556, ...), kind=kOutput, calls=%fused_computation.68.clone.1 | convolution fusion | flops 171442176 | bytes 950400 | tf_op jit(solution)/shard_map/while/body/tki,tij->tkj/dot_general | solution.py:100
  59.3 6.1 %fusion.457 = f32[32,26,128]{2,1,0:T(8,128)S(1)} fusion(f32[32,26,128]{2,1,0:T(8,128)S(1)} %gather_fusion, f32[32]{0:T(128)S(1)} %fusion.454, f32[32,128]{1,0:T(8,128)S(1)} %bitcast.559, f32[32,128]{1,0:T(8,128)S(1)} %bitcast.595, f32[32,128]{1,0:T(8,128)S(1)} %bitcast.557, f32[32,128]{1,0:T(8,128)S(1)} %bitcast.593, f32[32,128]{1,0:T(8,128)S(1)} %bitcast.555, ...), kind=kOutput, calls=%fused_computation.69.clone.1 | convolution fusion | flops 171442176 | bytes 950400 | tf_op jit(solution)/shard_map/while/body/tkj,tij->tki/dot_general | solution.py:96
  67.8 4.9 %fusion.458 = f32[32,26,128]{2,1,0:T(8,128)S(1)} fusion(f32[32,26,128]{2,1,0:T(8,128)S(1)} %gather_fusion.3, f32[32]{0:T(128)S(1)} %fusion.454, f32[32,128]{1,0:T(8,128)S(1)} %bitcast.560, f32[32,128]{1,0:T(8,128)S(1)} %bitcast.596, f32[32,128]{1,0:T(8,128)S(1)} %bitcast.558, f32[32,128]{1,0:T(8,128)S(1)} %bitcast.594, f32[32,128]{1,0:T(8,128)S(1)} %bitcast.556, ...), kind=kOutput, calls=%fused_computation.68.clone.1 | convolution fusion | flops 171442176 | bytes 950400 | tf_op jit(solution)/shard_map/while/body/tki,tij->tkj/dot_general | solution.py:100
  72.7 1.9 scatter_fusion.1
  77.2 6.1 %fusion.457 = f32[32,26,128]{2,1,0:T(8,128)S(1)} fusion(f32[32,26,128]{2,1,0:T(8,128)S(1)} %gather_fusion, f32[32]{0:T(128)S(1)} %fusion.454, f32[32,128]{1,0:T(8,128)S(1)} %bitcast.559, f32[32,128]{1,0:T(8,128)S(1)} %bitcast.595, f32[32,128]{1,0:T(8,128)S(1)} %bitcast.557, f32[32,128]{1,0:T(8,128)S(1)} %bitcast.593, f32[32,128]{1,0:T(8,128)S(1)} %bitcast.555, ...), kind=kOutput, calls=%fused_computation.69.clone.1 | convolution fusion | flops 171442176 | bytes 950400 | tf_op jit(solution)/shard_map/while/body/tkj,tij->tki/dot_general | solution.py:96
  85.8 4.9 %fusion.458 = f32[32,26,128]{2,1,0:T(8,128)S(1)} fusion(f32[32,26,128]{2,1,0:T(8,128)S(1)} %gather_fusion.3, f32[32]{0:T(128)S(1)} %fusion.454, f32[32,128]{1,0:T(8,128)S(1)} %bitcast.560, f32[32,128]{1,0:T(8,128)S(1)} %bitcast.596, f32[32,128]{1,0:T(8,128)S(1)} %bitcast.558, f32[32,128]{1,0:T(8,128)S(1)} %bitcast.594, f32[32,128]{1,0:T(8,128)S(1)} %bitcast.556, ...), kind=kOutput, calls=%fused_computation.68.clone.1 | convolution fusion | flops 171442176 | bytes 950400 | tf_op jit(solution)/shard_map/while/body/tki,tij->tkj/dot_general | solution.py:100
  90.7 1.9 scatter_fusion.1
  95.3 34.7 %while.91 = (s32[]{:T(128)}, f32[16,26,128]{2,1,0:T(8,128)S(1)}, f32[16,26,128]{2,1,0:T(8,128)S(1)}, s32[64,2]{0,1:T(2,128)S(1)}, f32[16,26,128]{2,1,0:T(8,128)S...) while((s32[]{:T(128)}, f32[16,26,128]{2,1,0:T(8,128)S(1)}, ...), condition=%wide.region_7.8_spmd.clone, body=%wide.region_4.7_spmd.clone.sunk | while | flops 343099680 | bytes 6564403 | solution.py:111
  97.3 6.1 %fusion.466 = f32[32,26,128]{2,1,0:T(8,128)S(1)} fusion(f32[32,26,128]{2,1,0:T(8,128)S(1)} %gather_fusion.4, f32[32]{0:T(128)S(1)} %compare_select_fusion.28, f32[32,128]{1,0:T(8,128)S(1)} %bitcast.565, f32[32,128]{1,0:T(8,128)S(1)} %bitcast.601, f32[32,128]{1,0:T(8,128)S(1)} %bitcast.563, f32[32,128]{1,0:T(8,128)S(1)} %bitcast.599, ...), kind=kOutput, calls=%fused_computation.115.clone.1 | convolution fusion | flops 171442176 | bytes 950400 | tf_op jit(solution)/shard_map/while/body/eval_jaxpr/tkj,tij->tki/dot_general | solution.py:96
  103.4 1.9 scatter_fusion.2
  105.8 4.9 %fusion.467 = f32[32,26,128]{2,1,0:T(8,128)S(1)} fusion(f32[32,26,128]{2,1,0:T(8,128)S(1)} %gather_fusion.7, f32[32]{0:T(128)S(1)} %compare_select_fusion.28, f32[32,128]{1,0:T(8,128)S(1)} %bitcast.566, f32[32,128]{1,0:T(8,128)S(1)} %bitcast.602, f32[32,128]{1,0:T(8,128)S(1)} %bitcast.564, f32[32,128]{1,0:T(8,128)S(1)} %bitcast.600, ...), kind=kOutput, calls=%fused_computation.114.clone.1 | convolution fusion | flops 171442176 | bytes 950400 | tf_op jit(solution)/shard_map/while/body/eval_jaxpr/tki,tij->tkj/dot_general | solution.py:100
  110.8 1.9 scatter_fusion.3
  114.6 6.1 %fusion.466 = f32[32,26,128]{2,1,0:T(8,128)S(1)} fusion(f32[32,26,128]{2,1,0:T(8,128)S(1)} %gather_fusion.4, f32[32]{0:T(128)S(1)} %compare_select_fusion.28, f32[32,128]{1,0:T(8,128)S(1)} %bitcast.565, f32[32,128]{1,0:T(8,128)S(1)} %bitcast.601, f32[32,128]{1,0:T(8,128)S(1)} %bitcast.563, f32[32,128]{1,0:T(8,128)S(1)} %bitcast.599, ...), kind=kOutput, calls=%fused_computation.115.clone.1 | convolution fusion | flops 171442176 | bytes 950400 | tf_op jit(solution)/shard_map/while/body/eval_jaxpr/tkj,tij->tki/dot_general | solution.py:96
  120.7 1.9 scatter_fusion.2
  123.2 4.9 %fusion.467 = f32[32,26,128]{2,1,0:T(8,128)S(1)} fusion(f32[32,26,128]{2,1,0:T(8,128)S(1)} %gather_fusion.7, f32[32]{0:T(128)S(1)} %compare_select_fusion.28, f32[32,128]{1,0:T(8,128)S(1)} %bitcast.566, f32[32,128]{1,0:T(8,128)S(1)} %bitcast.602, f32[32,128]{1,0:T(8,128)S(1)} %bitcast.564, f32[32,128]{1,0:T(8,128)S(1)} %bitcast.600, ...), kind=kOutput, calls=%fused_computation.114.clone.1 | convolution fusion | flops 171442176 | bytes 950400 | tf_op jit(solution)/shard_map/while/body/eval_jaxpr/tki,tij->tkj/dot_general | solution.py:100
  128.1 1.9 scatter_fusion.3
  130.0 1.9 collective-permute-start.1
  133.8 34.7 %while.92 = (s32[]{:T(128)}, f32[16,26,128]{2,1,0:T(8,128)S(1)}, f32[16,26,128]{2,1,0:T(8,128)S(1)}, s32[64,2]{0,1:T(2,128)S(1)}, f32[16,26,128]{2,1,0:T(8,128)S...) while((s32[]{:T(128)}, f32[16,26,128]{2,1,0:T(8,128)S(1)}, ...), condition=%wide.region_13.14_spmd.clone, body=%wide.region_10.13_spmd.clone.sunk | while | flops 343099680 | bytes 6564403 | solution.py:111
  135.8 6.1 %fusion.475 = f32[32,26,128]{2,1,0:T(8,128)S(1)} fusion(f32[32,26,128]{2,1,0:T(8,128)S(1)} %gather_fusion.8, f32[32]{0:T(128)S(1)} %compare_select_fusion.29, f32[32,128]{1,0:T(8,128)S(1)} %bitcast.571, f32[32,128]{1,0:T(8,128)S(1)} %bitcast.607, f32[32,128]{1,0:T(8,128)S(1)} %bitcast.569, f32[32,128]{1,0:T(8,128)S(1)} %bitcast.605, ...), kind=kOutput, calls=%fused_computation.158.clone.1 | convolution fusion | flops 171442176 | bytes 950400 | tf_op jit(solution)/shard_map/while/body/eval_jaxpr/tkj,tij->tki/dot_general | solution.py:96
  141.9 1.9 scatter_fusion.4
  144.3 4.9 %fusion.476 = f32[32,26,128]{2,1,0:T(8,128)S(1)} fusion(f32[32,26,128]{2,1,0:T(8,128)S(1)} %gather_fusion.11, f32[32]{0:T(128)S(1)} %compare_select_fusion.29, f32[32,128]{1,0:T(8,128)S(1)} %bitcast.572, f32[32,128]{1,0:T(8,128)S(1)} %bitcast.608, f32[32,128]{1,0:T(8,128)S(1)} %bitcast.570, f32[32,128]{1,0:T(8,128)S(1)} %bitcast.606, ...), kind=kOutput, calls=%fused_computation.157.clone.1 | convolution fusion | flops 171442176 | bytes 950400 | tf_op jit(solution)/shard_map/while/body/eval_jaxpr/tki,tij->tkj/dot_general | solution.py:100
  149.3 1.8 scatter_fusion.5
  153.1 6.1 %fusion.475 = f32[32,26,128]{2,1,0:T(8,128)S(1)} fusion(f32[32,26,128]{2,1,0:T(8,128)S(1)} %gather_fusion.8, f32[32]{0:T(128)S(1)} %compare_select_fusion.29, f32[32,128]{1,0:T(8,128)S(1)} %bitcast.571, f32[32,128]{1,0:T(8,128)S(1)} %bitcast.607, f32[32,128]{1,0:T(8,128)S(1)} %bitcast.569, f32[32,128]{1,0:T(8,128)S(1)} %bitcast.605, ...), kind=kOutput, calls=%fused_computation.158.clone.1 | convolution fusion | flops 171442176 | bytes 950400 | tf_op jit(solution)/shard_map/while/body/eval_jaxpr/tkj,tij->tki/dot_general | solution.py:96
  159.2 1.9 scatter_fusion.4
  161.7 4.9 %fusion.476 = f32[32,26,128]{2,1,0:T(8,128)S(1)} fusion(f32[32,26,128]{2,1,0:T(8,128)S(1)} %gather_fusion.11, f32[32]{0:T(128)S(1)} %compare_select_fusion.29, f32[32,128]{1,0:T(8,128)S(1)} %bitcast.572, f32[32,128]{1,0:T(8,128)S(1)} %bitcast.608, f32[32,128]{1,0:T(8,128)S(1)} %bitcast.570, f32[32,128]{1,0:T(8,128)S(1)} %bitcast.606, ...), kind=kOutput, calls=%fused_computation.157.clone.1 | convolution fusion | flops 171442176 | bytes 950400 | tf_op jit(solution)/shard_map/while/body/eval_jaxpr/tki,tij->tkj/dot_general | solution.py:100
  166.6 1.9 scatter_fusion.5
  170.0 1.9 scatter_fusion.13
  181.3 9.6 %collective-permute-start.4 = (f32[16,29,128]{2,1,0:T(8,128)S(1)}, f32[16,29,128]{2,1,0:T(8,128)S(1)}, u32[]{:S(2)}, u32[]{:S(2)}) collective-permute-start(f32[16,29,128]{2,1,0:T(8,128)S(1)} %pad_maximum_fusion.2), channel_id=1, source_target_pairs={{1,0},{2,1},{3,2},{4,3},{5,4},{6,5},{7,6},{8,7},{9,8},{10,9},{11,1... | collective-permute-start | bytes 712712 | tf_op jit(solution)/shard_map/ppermute | solution.py:30
  195.3 34.7 %while.94 = (s32[]{:T(128)}, f32[16,26,128]{2,1,0:T(8,128)S(1)}, f32[16,26,128]{2,1,0:T(8,128)S(1)}, s32[64,2]{0,1:T(2,128)S(1)}, f32[16,26,128]{2,1,0:T(8,128)S...) while((s32[]{:T(128)}, f32[16,26,128]{2,1,0:T(8,128)S(1)}, ...), condition=%wide.region_24.25_spmd.clone, body=%wide.region_21.24_spmd.clone.sunk | while | flops 343099680 | bytes 6564403 | solution.py:111
  197.3 6.1 %fusion.494 = f32[32,26,128]{2,1,0:T(8,128)S(1)} fusion(f32[32,26,128]{2,1,0:T(8,128)S(1)} %gather_fusion.16, f32[32]{0:T(128)S(1)} %compare_select_fusion.30, f32[32,128]{1,0:T(8,128)S(1)} %bitcast.577, f32[32,128]{1,0:T(8,128)S(1)} %bitcast.613, f32[32,128]{1,0:T(8,128)S(1)} %bitcast.575, f32[32,128]{1,0:T(8,128)S(1)} %bitcast.611, ...), kind=kOutput, calls=%fused_computation.247.clone.1 | convolution fusion | flops 171442176 | bytes 950400 | tf_op jit(solution)/shard_map/while/body/eval_jaxpr/tkj,tij->tki/dot_general | solution.py:96
  203.4 1.9 scatter_fusion.8
  205.9 4.9 %fusion.495 = f32[32,26,128]{2,1,0:T(8,128)S(1)} fusion(f32[32,26,128]{2,1,0:T(8,128)S(1)} %gather_fusion.19, f32[32]{0:T(128)S(1)} %compare_select_fusion.30, f32[32,128]{1,0:T(8,128)S(1)} %bitcast.578, f32[32,128]{1,0:T(8,128)S(1)} %bitcast.614, f32[32,128]{1,0:T(8,128)S(1)} %bitcast.576, f32[32,128]{1,0:T(8,128)S(1)} %bitcast.612, ...), kind=kOutput, calls=%fused_computation.246.clone.1 | convolution fusion | flops 171442176 | bytes 950400 | tf_op jit(solution)/shard_map/while/body/eval_jaxpr/tki,tij->tkj/dot_general | solution.py:100
  210.8 1.9 scatter_fusion.9
  214.6 6.1 %fusion.494 = f32[32,26,128]{2,1,0:T(8,128)S(1)} fusion(f32[32,26,128]{2,1,0:T(8,128)S(1)} %gather_fusion.16, f32[32]{0:T(128)S(1)} %compare_select_fusion.30, f32[32,128]{1,0:T(8,128)S(1)} %bitcast.577, f32[32,128]{1,0:T(8,128)S(1)} %bitcast.613, f32[32,128]{1,0:T(8,128)S(1)} %bitcast.575, f32[32,128]{1,0:T(8,128)S(1)} %bitcast.611, ...), kind=kOutput, calls=%fused_computation.247.clone.1 | convolution fusion | flops 171442176 | bytes 950400 | tf_op jit(solution)/shard_map/while/body/eval_jaxpr/tkj,tij->tki/dot_general | solution.py:96
  220.7 1.9 scatter_fusion.8
  223.2 4.9 %fusion.495 = f32[32,26,128]{2,1,0:T(8,128)S(1)} fusion(f32[32,26,128]{2,1,0:T(8,128)S(1)} %gather_fusion.19, f32[32]{0:T(128)S(1)} %compare_select_fusion.30, f32[32,128]{1,0:T(8,128)S(1)} %bitcast.578, f32[32,128]{1,0:T(8,128)S(1)} %bitcast.614, f32[32,128]{1,0:T(8,128)S(1)} %bitcast.576, f32[32,128]{1,0:T(8,128)S(1)} %bitcast.612, ...), kind=kOutput, calls=%fused_computation.246.clone.1 | convolution fusion | flops 171442176 | bytes 950400 | tf_op jit(solution)/shard_map/while/body/eval_jaxpr/tki,tij->tkj/dot_general | solution.py:100
  228.1 1.9 scatter_fusion.9
  230.0 1.9 collective-permute-start.5
  233.8 40.5 %while.95 = (s32[]{:T(128)}, f32[16,26,128]{2,1,0:T(8,128)S(1)}, f32[16,26,128]{2,1,0:T(8,128)S(1)}, s32[64,2]{0,1:T(2,128)S(1)}, f32[16,26,128]{2,1,0:T(8,128)S...) while((s32[]{:T(128)}, f32[16,26,128]{2,1,0:T(8,128)S(1)}, ...), condition=%wide.region_30.31_spmd.clone, body=%wide.region_27.30_spmd.clone.sunk | while | flops 343099680 | bytes 6630507 | solution.py:111
  237.0 6.7 %fusion.503 = f32[32,26,128]{2,1,0:T(8,128)S(1)} fusion(f32[32,26,128]{2,1,0:T(8,128)S(1)} %gather_fusion.20, f32[32]{0:T(128)} %compare_select_fusion.31, f32[32,128]{1,0:T(8,128)S(1)} %bitcast.583, f32[32,128]{1,0:T(8,128)S(1)} %bitcast.619, f32[32,128]{1,0:T(8,128)S(1)} %bitcast.581, f32[32,128]{1,0:T(8,128)S(1)} %bitcast.617, ...), kind=kOutput, calls=%fused_computation.290.clone.1 | convolution fusion | flops 171442176 | bytes 950400 | tf_op jit(solution)/shard_map/while/body/eval_jaxpr/tkj,tij->tki/dot_general | solution.py:96
  243.6 2.0 scatter_fusion.10
  246.2 5.9 %fusion.504 = f32[32,26,128]{2,1,0:T(8,128)S(1)} fusion(f32[32,26,128]{2,1,0:T(8,128)S(1)} %gather_fusion.23, f32[32]{0:T(128)} %compare_select_fusion.31, f32[32,128]{1,0:T(8,128)S(1)} %bitcast.584, f32[32,128]{1,0:T(8,128)} %bitcast.620, f32[32,128]{1,0:T(8,128)S(1)} %bitcast.582, f32[32,128]{1,0:T(8,128)S(1)} %bitcast.618, ...), kind=kOutput, calls=%fused_computation.289.clone.1 | convolution fusion | flops 171442176 | bytes 950400 | tf_op jit(solution)/shard_map/while/body/eval_jaxpr/tki,tij->tkj/dot_general | solution.py:100
  257.2 6.7 %fusion.503 = f32[32,26,128]{2,1,0:T(8,128)S(1)} fusion(f32[32,26,128]{2,1,0:T(8,128)S(1)} %gather_fusion.20, f32[32]{0:T(128)} %compare_select_fusion.31, f32[32,128]{1,0:T(8,128)S(1)} %bitcast.583, f32[32,128]{1,0:T(8,128)S(1)} %bitcast.619, f32[32,128]{1,0:T(8,128)S(1)} %bitcast.581, f32[32,128]{1,0:T(8,128)S(1)} %bitcast.617, ...), kind=kOutput, calls=%fused_computation.290.clone.1 | convolution fusion | flops 171442176 | bytes 950400 | tf_op jit(solution)/shard_map/while/body/eval_jaxpr/tkj,tij->tki/dot_general | solution.py:96
  263.8 2.0 scatter_fusion.10
  266.4 5.9 %fusion.504 = f32[32,26,128]{2,1,0:T(8,128)S(1)} fusion(f32[32,26,128]{2,1,0:T(8,128)S(1)} %gather_fusion.23, f32[32]{0:T(128)} %compare_select_fusion.31, f32[32,128]{1,0:T(8,128)S(1)} %bitcast.584, f32[32,128]{1,0:T(8,128)} %bitcast.620, f32[32,128]{1,0:T(8,128)S(1)} %bitcast.582, f32[32,128]{1,0:T(8,128)S(1)} %bitcast.618, ...), kind=kOutput, calls=%fused_computation.289.clone.1 | convolution fusion | flops 171442176 | bytes 950400 | tf_op jit(solution)/shard_map/while/body/eval_jaxpr/tki,tij->tkj/dot_general | solution.py:100
  272.4 1.9 scatter_fusion.11
  275.0 78.8 %while.93 = (s32[]{:T(128)}, f32[32,26,128]{2,1,0:T(8,128)S(1)}, f32[32,26,128]{2,1,0:T(8,128)S(1)}, s32[]{:T(128)}, s32[128,2]{0,1:T(2,128)S(1)}, /*index=5*/f3...) while((s32[]{:T(128)}, f32[32,26,128]{2,1,0:T(8,128)S(1)}, ...), condition=%wide.region_20.21_spmd.clone, body=%wide.region_17.20_spmd.clone.sunk | while | flops 343099776 | bytes 6564663 | solution.py:111
  278.7 6.1 %fusion.485 = f32[32,26,128]{2,1,0:T(8,128)S(1)} fusion(f32[32,26,128]{2,1,0:T(8,128)} %gather_fusion.12, f32[32]{0:T(128)S(1)} %fusion.482, f32[32,128]{1,0:T(8,128)S(1)} %bitcast.589, f32[32,128]{1,0:T(8,128)S(1)} %bitcast.625, f32[32,128]{1,0:T(8,128)S(1)} %bitcast.587, f32[32,128]{1,0:T(8,128)S(1)} %bitcast.623, f32[32,128]{1,0:T(8,128)S(1)} %bitcast.585, ...), kind=kOutput, calls=%fused_computation.201.clone.1 | convolution fusion | flops 171442176 | bytes 950400 | tf_op jit(solution)/shard_map/while/body/tkj,tij->tki/dot_general | solution.py:96
  288.1 4.9 %fusion.486 = f32[32,26,128]{2,1,0:T(8,128)S(1)} fusion(f32[32,26,128]{2,1,0:T(8,128)} %gather_fusion.15, f32[32]{0:T(128)S(1)} %fusion.482, f32[32,128]{1,0:T(8,128)S(1)} %bitcast.590, f32[32,128]{1,0:T(8,128)S(1)} %bitcast.626, f32[32,128]{1,0:T(8,128)S(1)} %bitcast.588, f32[32,128]{1,0:T(8,128)S(1)} %bitcast.624, f32[32,128]{1,0:T(8,128)S(1)} %bitcast.586, ...), kind=kOutput, calls=%fused_computation.200.clone.1 | convolution fusion | flops 171442176 | bytes 950400 | tf_op jit(solution)/shard_map/while/body/tki,tij->tkj/dot_general | solution.py:100
  298.4 6.1 %fusion.485 = f32[32,26,128]{2,1,0:T(8,128)S(1)} fusion(f32[32,26,128]{2,1,0:T(8,128)} %gather_fusion.12, f32[32]{0:T(128)S(1)} %fusion.482, f32[32,128]{1,0:T(8,128)S(1)} %bitcast.589, f32[32,128]{1,0:T(8,128)S(1)} %bitcast.625, f32[32,128]{1,0:T(8,128)S(1)} %bitcast.587, f32[32,128]{1,0:T(8,128)S(1)} %bitcast.623, f32[32,128]{1,0:T(8,128)S(1)} %bitcast.585, ...), kind=kOutput, calls=%fused_computation.201.clone.1 | convolution fusion | flops 171442176 | bytes 950400 | tf_op jit(solution)/shard_map/while/body/tkj,tij->tki/dot_general | solution.py:96
  307.7 4.9 %fusion.486 = f32[32,26,128]{2,1,0:T(8,128)S(1)} fusion(f32[32,26,128]{2,1,0:T(8,128)} %gather_fusion.15, f32[32]{0:T(128)S(1)} %fusion.482, f32[32,128]{1,0:T(8,128)S(1)} %bitcast.590, f32[32,128]{1,0:T(8,128)S(1)} %bitcast.626, f32[32,128]{1,0:T(8,128)S(1)} %bitcast.588, f32[32,128]{1,0:T(8,128)S(1)} %bitcast.624, f32[32,128]{1,0:T(8,128)S(1)} %bitcast.586, ...), kind=kOutput, calls=%fused_computation.200.clone.1 | convolution fusion | flops 171442176 | bytes 950400 | tf_op jit(solution)/shard_map/while/body/tki,tij->tkj/dot_general | solution.py:100
  318.0 6.1 %fusion.485 = f32[32,26,128]{2,1,0:T(8,128)S(1)} fusion(f32[32,26,128]{2,1,0:T(8,128)} %gather_fusion.12, f32[32]{0:T(128)S(1)} %fusion.482, f32[32,128]{1,0:T(8,128)S(1)} %bitcast.589, f32[32,128]{1,0:T(8,128)S(1)} %bitcast.625, f32[32,128]{1,0:T(8,128)S(1)} %bitcast.587, f32[32,128]{1,0:T(8,128)S(1)} %bitcast.623, f32[32,128]{1,0:T(8,128)S(1)} %bitcast.585, ...), kind=kOutput, calls=%fused_computation.201.clone.1 | convolution fusion | flops 171442176 | bytes 950400 | tf_op jit(solution)/shard_map/while/body/tkj,tij->tki/dot_general | solution.py:96
  327.4 4.9 %fusion.486 = f32[32,26,128]{2,1,0:T(8,128)S(1)} fusion(f32[32,26,128]{2,1,0:T(8,128)} %gather_fusion.15, f32[32]{0:T(128)S(1)} %fusion.482, f32[32,128]{1,0:T(8,128)S(1)} %bitcast.590, f32[32,128]{1,0:T(8,128)S(1)} %bitcast.626, f32[32,128]{1,0:T(8,128)S(1)} %bitcast.588, f32[32,128]{1,0:T(8,128)S(1)} %bitcast.624, f32[32,128]{1,0:T(8,128)S(1)} %bitcast.586, ...), kind=kOutput, calls=%fused_computation.200.clone.1 | convolution fusion | flops 171442176 | bytes 950400 | tf_op jit(solution)/shard_map/while/body/tki,tij->tkj/dot_general | solution.py:100
  332.3 1.9 scatter_fusion.7
  337.7 6.1 %fusion.485 = f32[32,26,128]{2,1,0:T(8,128)S(1)} fusion(f32[32,26,128]{2,1,0:T(8,128)} %gather_fusion.12, f32[32]{0:T(128)S(1)} %fusion.482, f32[32,128]{1,0:T(8,128)S(1)} %bitcast.589, f32[32,128]{1,0:T(8,128)S(1)} %bitcast.625, f32[32,128]{1,0:T(8,128)S(1)} %bitcast.587, f32[32,128]{1,0:T(8,128)S(1)} %bitcast.623, f32[32,128]{1,0:T(8,128)S(1)} %bitcast.585, ...), kind=kOutput, calls=%fused_computation.201.clone.1 | convolution fusion | flops 171442176 | bytes 950400 | tf_op jit(solution)/shard_map/while/body/tkj,tij->tki/dot_general | solution.py:96
  347.0 4.9 %fusion.486 = f32[32,26,128]{2,1,0:T(8,128)S(1)} fusion(f32[32,26,128]{2,1,0:T(8,128)} %gather_fusion.15, f32[32]{0:T(128)S(1)} %fusion.482, f32[32,128]{1,0:T(8,128)S(1)} %bitcast.590, f32[32,128]{1,0:T(8,128)S(1)} %bitcast.626, f32[32,128]{1,0:T(8,128)S(1)} %bitcast.588, f32[32,128]{1,0:T(8,128)S(1)} %bitcast.624, f32[32,128]{1,0:T(8,128)S(1)} %bitcast.586, ...), kind=kOutput, calls=%fused_computation.200.clone.1 | convolution fusion | flops 171442176 | bytes 950400 | tf_op jit(solution)/shard_map/while/body/tki,tij->tkj/dot_general | solution.py:100
  352.0 1.9 scatter_fusion.7
  355.7 1.9 scatter_fusion.17
  358.9 1.9 scatter_fusion.19
  (402 shorter events, 116.2 us)
Async XLA Ops:
  0.6 1.7 copy-start.11
  0.6 1.7 copy-start
  0.7 1.6 copy-start.1
  1.5 1.1 copy-start.18
  1.5 1.1 copy-start.4
  2.6 1.4 copy-start.2
  4.3 0.7 copy-start.29
  4.9 163.8 %copy-start.27 = (s32[16]{0:T(128)}, s32[16]{0:T(128)S(1)}, u32[]{:S(2)}) copy-start(s32[16]{0:T(128)S(1)} %get-tuple-element.1222) | copy-start | bytes 196
  4.9 165.0 %copy-start.25 = (s32[16]{0:T(128)}, s32[16]{0:T(128)S(1)}, u32[]{:S(2)}) copy-start(s32[16]{0:T(128)S(1)} %get-tuple-element.1221) | copy-start | bytes 196
  5.0 167.0 %copy-start.23 = (s32[16]{0:T(128)}, s32[16]{0:T(128)S(1)}, u32[]{:S(2)}) copy-start(s32[16]{0:T(128)S(1)} %get-tuple-element.1223) | copy-start | bytes 196
  5.0 169.6 %copy-start.21 = (s32[16]{0:T(128)}, s32[16]{0:T(128)S(1)}, u32[]{:S(2)}) copy-start(s32[16]{0:T(128)S(1)} %get-tuple-element.1220) | copy-start | bytes 196
  6.9 88.3 %collective-permute-start = (f32[16,29,128]{2,1,0:T(8,128)}, f32[16,29,128]{2,1,0:T(8,128)S(1)}, u32[]{:S(2)}, u32[]{:S(2)}) collective-permute-start(f32[16,29,128]{2,1,0:T(8,128)} %pad_maximum_fusion), channel_id=1, source_target_pairs={{1,0},{2,1},{3,2},{4,3},{5,4},{6,5},{7,6},{8,7},{9,8},{10,9},{11,1... | collective-permute-start | bytes 712712 | tf_op jit(solution)/shard_map/ppermute | solution.py:30
  19.4 112.5 %collective-permute-start.2 = (f32[16,29,128]{2,1,0:T(8,128)}, f32[16,29,128]{2,1,0:T(8,128)}, u32[]{:S(2)}, u32[]{:S(2)}) collective-permute-start(f32[16,29,128]{2,1,0:T(8,128)} %pad_maximum_fusion.1), channel_id=1, source_target_pairs={{0,192},{64,0},{128,64},{192,128},{1,193},{65,1},{129,65},{193,129... | collective-permute-start | bytes 712712 | tf_op jit(solution)/shard_map/ppermute | solution.py:36
  20.1 0.7 copy-start.16
  20.7 71.8 %copy-start.30 = (s32[1,1,2,48,2]{3,4,2,1,0:T(2,128)S(1)}, s32[1,1,2,48,2]{3,4,2,1,0:T(2,128)}, u32[]{:S(2)}) copy-start(s32[1,1,2,48,2]{3,4,2,1,0:T(2,128)} %param.36) | copy-start | bytes 2308
  20.8 71.8 %copy-start.31 = (s32[1,1,16]{2,1,0:T(1,128)S(1)}, s32[1,1,16]{2,1,0:T(1,128)}, u32[]{:S(2)}) copy-start(s32[1,1,16]{2,1,0:T(1,128)} %param.37) | copy-start | bytes 196
  95.2 81.7 %copy-start.13 = (f32[32,128]{1,0:T(8,128)}, f32[32,128]{1,0:T(8,128)S(1)}, u32[]{:S(2)}) copy-start(f32[32,128]{1,0:T(8,128)S(1)} %fusion.351) | copy-start | bytes 49156
  130.0 40.0 %collective-permute-start.1 = (f32[16,26,128]{2,1,0:T(8,128)S(1)}, f32[16,26,128]{2,1,0:T(8,128)}, u32[]{:S(2)}, u32[]{:S(2)}) collective-permute-start(f32[16,26,128]{2,1,0:T(8,128)S(1)} %get-tuple-element.725), channel_id=1, source_target_pairs={{0,1},{1,2},{2,3},{3,4},{4,5},{5,6},{6,7},{7,8},{8,9},{9,10},{10,1... | collective-permute-start | bytes 638984 | tf_op jit(solution)/shard_map/ppermute | solution.py:30
  168.5 6.1 %collective-permute-start.3 = (f32[16,26,128]{2,1,0:T(8,128)S(1)}, f32[16,26,128]{2,1,0:T(8,128)S(1)}, u32[]{:S(2)}, u32[]{:S(2)}) collective-permute-start(f32[16,26,128]{2,1,0:T(8,128)S(1)} %get-tuple-element.727), channel_id=1, source_target_pairs={{0,64},{64,128},{128,192},{192,0},{1,65},{65,129},{129,193},{193,1... | collective-permute-start | bytes 638984 | tf_op jit(solution)/shard_map/ppermute | solution.py:36
  168.8 8.0 %copy-start.19 = (f32[32]{0:T(128)}, f32[32]{0:T(128)S(1)}, u32[]{:S(2)}) copy-start(f32[32]{0:T(128)S(1)} %broadcast_multiply_fusion) | copy-start | bytes 388
  175.7 0.9 copy-start.10
  176.6 1.0 copy-start.3
  176.7 1.2 copy-start.5
  176.9 1.1 copy-start.7
  176.9 1.1 copy-start.8
  181.3 13.9 %collective-permute-start.4 = (f32[16,29,128]{2,1,0:T(8,128)S(1)}, f32[16,29,128]{2,1,0:T(8,128)S(1)}, u32[]{:S(2)}, u32[]{:S(2)}) collective-permute-start(f32[16,29,128]{2,1,0:T(8,128)S(1)} %pad_maximum_fusion.2), channel_id=1, source_target_pairs={{1,0},{2,1},{3,2},{4,3},{5,4},{6,5},{7,6},{8,7},{9,8},{10,9},{11,1... | collective-permute-start | bytes 712712 | tf_op jit(solution)/shard_map/ppermute | solution.py:30
  195.2 36.7 %collective-permute-start.6 = (f32[16,29,128]{2,1,0:T(8,128)}, f32[16,29,128]{2,1,0:T(8,128)}, u32[]{:S(2)}, u32[]{:S(2)}) collective-permute-start(f32[16,29,128]{2,1,0:T(8,128)} %pad_maximum_fusion.3), channel_id=1, source_target_pairs={{0,192},{64,0},{128,64},{192,128},{1,193},{65,1},{129,65},{193,129... | collective-permute-start | bytes 712712 | tf_op jit(solution)/shard_map/ppermute | solution.py:36
  230.0 125.7 %collective-permute-start.5 = (f32[16,26,128]{2,1,0:T(8,128)S(1)}, f32[16,26,128]{2,1,0:T(8,128)}, u32[]{:S(2)}, u32[]{:S(2)}) collective-permute-start(f32[16,26,128]{2,1,0:T(8,128)S(1)} %get-tuple-element.731), channel_id=1, source_target_pairs={{0,1},{1,2},{2,3},{3,4},{4,5},{5,6},{6,7},{7,8},{8,9},{9,10},{10,1... | collective-permute-start | bytes 638984 | tf_op jit(solution)/shard_map/ppermute | solution.py:30
  233.9 1.1 copy-start.15
  236.3 0.6 copy-start.12
  254.1 1.1 copy-start.15
  256.6 0.6 copy-start.12
  274.3 0.7 copy-start.17
  274.3 84.6 %collective-permute-start.7 = (f32[16,26,128]{2,1,0:T(8,128)S(1)}, f32[16,26,128]{2,1,0:T(8,128)}, u32[]{:S(2)}, u32[]{:S(2)}) collective-permute-start(f32[16,26,128]{2,1,0:T(8,128)S(1)} %get-tuple-element.733), channel_id=1, source_target_pairs={{0,64},{64,128},{128,192},{192,0},{1,65},{65,129},{129,193},{193,1... | collective-permute-start | bytes 638984 | tf_op jit(solution)/shard_map/ppermute | solution.py:36
  353.9 0.7 copy-start.28
  354.0 1.8 copy-start.26
  355.7 2.0 copy-start.24
  357.7 1.2 copy-start.22
  360.9 0.9 copy-start.6
  362.6 0.7 copy-start.14
  362.7 1.3 copy-start.9
  362.7 1.3 copy-start.20
where the time goes:
time: 366 us; the launch traced here: 365 us
  matrix products  179 us (49%)
  other arithmetic  88.6 us (24%)
  local copies, waits for them, and re-layouts  66.8 us (18%)
  starting transfers between devices  25 us (7%)
    dot_general x16, matrix products, one_group(): jnp.einsum('tkj,tij->tki', col_sources[col_block], kernel, precision=lax....  98.5 us
    dot_general x16, matrix products, one_group(): jnp.einsum('tki,tij->tkj', row_sources[row_block], kernel, precision=lax....  80.6 us
    scatter-add x16, other arithmetic, one_group(): row_summed = row_summed.at[row_block].add(to_rows)  29.9 us
    scatter-add x16, other arithmetic, one_group(): col_summed = col_summed.at[col_block].add(to_cols)  29.7 us
    ppermute x4, starting transfers between devices, from_behind(): return lax.ppermute(block, axis, route)  24.1 us
    gather x32, local copies, waits for them, and re-layouts, one_group(): kernel = pair_kernel(row_places[row_block], col_places[col_block], weight)  19.5 us
    gather x16, local copies, waits for them, and re-layouts, one_group(): row_sources[row_block]  12.6 us
    gather x16, local copies, waits for them, and re-layouts, one_group(): col_sources[col_block]  12.6 us
  transfers between devices with their start and end apart: 8, of which 1 were waited for; matrix products, arithmetic and copies ran while one was open for 86% of the time, Pallas kernels for 0%

commit v1 on v0

v1 whole, which is shorter than its diff:
```python
import functools

import jax
import jax.numpy as jnp
from jax import lax
from jax.experimental import pallas as pl
from jax.experimental.pallas import tpu as pltpu
from jax.sharding import PartitionSpec as P

RETURN_ITERS = 4
ROWS = 16
GROUP = 16

smooth_len = 1.5
kernel_coef = -105.0 / (3.141592653589793 * 1.5**5)
time_step = 0.25
gravity = 1.0
spin_rate = 2.0
blade_stiff = 4.0
bulk_mod = 2.0
shear_mod = 1.5
friction = 0.25
harden_scale = 0.05
harden_mod = 0.5
relax_rate = 0.7
tau_floor = 0.5
voigt_index = ((0, 3, 5), (3, 1, 4), (5, 4, 2))
voigt_pairs = ((0, 0), (1, 1), (2, 2), (0, 1), (1, 2), (0, 2))
bf16 = jnp.bfloat16
f32 = jnp.float32


def by_axis(value, axis, steps, closed):
    count = lax.axis_size(axis)
    pairs = [(i, (i + steps) % count) for i in range(count)]
    if not closed:
        pairs = [(i, j) for i, j in pairs if j == i + steps]
    return lax.ppermute(value, axis, pairs)


def halves(value):
    high = value.astype(bf16).astype(f32)
    return high, value - high


def source_rows(row):
    places = [row(k) for k in range(3)]
    motion = [row(3 + k) for k in range(3)]
    scaled = [row(6 + k) for k in range(6)]
    mass, volume = row(12), row(13)
    out = [mass]
    out += [mass * x for x in places]
    out += [mass * s for s in scaled]
    for k in range(3):
        dotted = scaled[voigt_index[k][0]] * places[0]
        dotted = dotted + scaled[voigt_index[k][1]] * places[1]
        dotted = dotted + scaled[voigt_index[k][2]] * places[2]
        out.append(mass * dotted)
    out.append(volume)
    out += [volume * v for v in motion]
    out += [volume * x for x in places]
    for a, b in voigt_pairs:
        out.append(volume * (0.5 * (motion[a] * places[b] + motion[b] * places[a])))
    return out


def distance_rows(row):
    places = [row(k) * (1.0 / smooth_len) for k in range(3)]
    square = places[0] * places[0] + places[1] * places[1] + places[2] * places[2]
    high, low = zip(*[halves(x) for x in places])
    n0, rest = halves(square)
    n1, n2 = halves(rest)
    one = jnp.ones_like(square)
    zero = jnp.zeros_like(square)
    from_side = [-2.0 * x for x in high + low + high] + [n0, n1, n2, one, one, one, zero]
    to_side = list(high + high + low) + [one, one, one, n0, n1, n2, zero]
    return from_side, to_side


def build_tables(row, base, count, src32, far32, S_ref, A_ref, to32, B_ref):
    for f, value in enumerate(source_rows(row)):
        src32[pl.ds(base * 32 + f, count, stride=32), :] = value
    from_side, to_side = distance_rows(row)
    for f, value in enumerate(from_side):
        far32[pl.ds(base * 16 + f, count, stride=16), :] = value
    if B_ref is not None:
        for f, value in enumerate(to_side):
            to32[pl.ds(base * 16 + f, count, stride=16), :] = value


def finish_tables(total, src32, far32, S_ref, A_ref, to32, B_ref):
    unroll = 4

    def some(i, carry):
        for u in range(unroll):
            b = i * unroll + u
            value = src32[pl.ds(pl.multiple_of(b * 32, 32), 32), :]
            high = value.astype(bf16)
            S_ref[b, 0:32, :] = high
            S_ref[b, 32:64, :] = (value - high.astype(f32)).astype(bf16)
            A_ref[b] = far32[pl.ds(pl.multiple_of(b * 16, 16), 16), :].T.astype(bf16)
            if B_ref is not None:
                B_ref[b] = to32[pl.ds(pl.multiple_of(b * 16, 16), 16), :].astype(bf16)
        return carry

    lax.fori_loop(0, total // unroll, some, 0)


def closeness_cubed(square):
    square = jnp.maximum(square, 1e-30)
    close = jnp.maximum(1.0 - square * lax.rsqrt(square), 0.0)
    return close * close * close


def tile_loop(item, groups, S_ref, A_ref, B_ref, acc_ref):
    def one_group(g, carry):
        outs = []
        for u in range(GROUP):
            target, source = item(g, u)
            square = jnp.dot(A_ref[source], B_ref[target[0]], preferred_element_type=f32)
            kernel = closeness_cubed(square)
            high = kernel.astype(bf16)
            low = (kernel - high.astype(f32)).astype(bf16)
            rows = S_ref[source]
            both = jnp.dot(
                jnp.concatenate([rows, rows], 1),
                jnp.concatenate([high, low], 0),
                preferred_element_type=f32,
            )
            outs.append((target[1], both[:32] + both[32:]))
        for target, value in outs:
            acc_ref[target] += value
        return carry

    lax.fori_loop(0, groups, one_group, 0)


def lanes_to_column(values):
    n = values.shape[1]
    rows = lax.broadcasted_iota(jnp.int32, (n, n), 0)
    cols = lax.broadcasted_iota(jnp.int32, (n, n), 1)
    return jnp.sum(jnp.where(rows == cols, values, 0.0), axis=1, keepdims=True)


def gather_rims(send_ref, state_ref, msgs):
    for face in range(4):
        for slot in range(16):
            block = send_ref[face, slot]
            msgs[face][pl.ds(slot, ROWS, stride=16), :] = state_ref[
                pl.ds(block, ROWS, stride=32), :
            ]


def start_kernel(send_ref, counts_ref, pos_ref, vel_ref, sig_ref, mass_ref, dens_ref, state_ref, *msgs):
    column = lanes_to_column(counts_ref[...].astype(f32))
    lane = lax.broadcasted_iota(jnp.int32, (32, 128), 1).astype(f32)
    mass = jnp.where(lane < column, mass_ref[...], 0.0)
    dens = dens_ref[...]
    state_ref[0:96, :] = pos_ref[...]
    state_ref[96:192, :] = vel_ref[...]
    square = dens * dens
    for k in range(6):
        state_ref[192 + 32 * k : 224 + 32 * k, :] = sig_ref[32 * k : 32 * k + 32, :] / square
    state_ref[384:416, :] = mass
    state_ref[416:448, :] = mass / dens
    state_ref[448:512, :] = jnp.zeros((64, 128), f32)
    gather_rims(send_ref, state_ref, msgs)


def own_kernel(count_ref, pairs_ref, state_ref, acc_ref, B_ref, S_ref, A_ref, src32, far32, to32, acc33):
    def row(k):
        return state_ref[32 * k : 32 * k + 32, :]

    build_tables(row, 0, 32, src32, far32, S_ref, A_ref, to32, B_ref)
    finish_tables(32, src32, far32, S_ref, A_ref, to32, B_ref)
    acc33[...] = jnp.zeros_like(acc33)
    total = count_ref[0]

    def item(g, u):
        q = g * (GROUP // 2) + u // 2
        a = pairs_ref[q, 0]
        b = pairs_ref[q, 1]
        live = q < total
        if u % 2 == 0:
            return (a, jnp.where(live, a, 32)), b
        return (b, jnp.where(jnp.logical_and(live, a != b), b, 32)), a

    groups = (total + GROUP // 2 - 1) // (GROUP // 2)
    tile_loop(item, groups, S_ref, A_ref, B_ref, acc33)
    acc_ref[...] = acc33[0:32]


def cross_terms(send_ref, link_ref, back_depth, back_strip, msgs, B_ref, S_ref, A_ref, src32, far32, acc):
    for face in range(4):
        def row(k, face=face):
            return msgs[face][16 * k : 16 * k + 16, :]

        build_tables(row, 16 * face, 16, src32, far32, S_ref, A_ref, None, None)
    finish_tables(64, src32, far32, S_ref, A_ref, None, None)
    acc[...] = jnp.zeros_like(acc)

    def item(g, u):
        q = g * (GROUP // 4) + u // 4
        if u % 4 == 0:
            target = send_ref[0, link_ref[0, q, 0]]
            source = link_ref[0, q, 1]
        elif u % 4 == 1:
            target = send_ref[1, back_depth[q, 1]]
            source = 16 + back_depth[q, 0]
        elif u % 4 == 2:
            target = send_ref[2, link_ref[1, q, 0]]
            source = 32 + link_ref[1, q, 1]
        else:
            target = send_ref[3, back_strip[q, 1]]
            source = 48 + back_strip[q, 0]
        return (target, target), source

    tile_loop(item, 48 // (GROUP // 4), S_ref, A_ref, B_ref, acc)


def rates(state_ref, own_acc, acc, flag, c):
    def total(f):
        at = pl.ds(8 * c * 32 + f, 8, stride=32)
        return kernel_coef * (own_acc[at, :] + acc[at, :])

    def row(k):
        return state_ref[32 * k + 8 * c : 32 * k + 8 * c + 8, :]

    places = [row(k) for k in range(3)]
    motion = [row(3 + k) for k in range(3)]
    scaled = [row(6 + k) for k in range(6)]
    blade = (spin_rate * places[2], jnp.zeros_like(places[1]), -spin_rate * places[0])
    mass_sum = total(0)
    lever = [places[l] * mass_sum - total(1 + l) for l in range(3)]
    stress_sum = [total(4 + s) for s in range(6)]
    acceleration = []
    for k in range(3):
        force = jnp.zeros_like(mass_sum)
        for l in range(3):
            slot = voigt_index[k][l]
            force = force + scaled[slot] * lever[l]
            force = force + places[l] * stress_sum[slot]
        force = force - total(10 + k)
        force = force + blade_stiff * flag * (blade[k] - motion[k])
        if k == 2:
            force = force - gravity
        acceleration.append(force)
    volume_sum = total(13)
    motion_sum = [total(14 + k) for k in range(3)]
    place_sum = [total(17 + k) for k in range(3)]
    strain = []
    for comp, (a, b) in enumerate(voigt_pairs):
        rate = 0.5 * (places[b] * motion_sum[a] + places[a] * motion_sum[b])
        rate = rate - total(20 + comp)
        rate = rate - 0.5 * volume_sum * (motion[a] * places[b] + motion[b] * places[a])
        rate = rate + 0.5 * (motion[a] * place_sum[b] + motion[b] * place_sum[a])
        strain.append(rate)
    return acceleration, strain


def elastic_step(stress, strain, fraction):
    volumetric = strain[0] + strain[1] + strain[2]
    lame_first = bulk_mod - 2.0 * shear_mod / 3.0
    components = []
    for comp in range(6):
        change = 2.0 * shear_mod * strain[comp]
        if comp < 3:
            change = change + lame_first * volumetric
        components.append(stress[comp] + fraction * time_step * change)
    return components


def plastic_return(components, plastic, cohesion):
    for _ in range(RETURN_ITERS):
        mean = (components[0] + components[1] + components[2]) / 3.0
        dev = [components[k] - mean for k in range(3)] + list(components[3:])
        second = 0.5 * (dev[0] * dev[0] + dev[1] * dev[1] + dev[2] * dev[2])
        second = second + dev[3] * dev[3] + dev[4] * dev[4] + dev[5] * dev[5]
        shear = jnp.sqrt(second)
        limit = cohesion * (1.0 + plastic / (plastic + harden_scale))
        excess = jnp.maximum(shear + friction * 3.0 * mean - limit, 0.0)
        multiplier = (relax_rate / (shear_mod + 9.0 * bulk_mod * friction * friction + harden_mod)) * excess
        shrink = jnp.maximum(1.0 - shear_mod * multiplier / jnp.maximum(shear, tau_floor), 0.0)
        mean = mean - 3.0 * bulk_mod * friction * multiplier
        components = [dev[k] * shrink + mean for k in range(3)] + [dev[k] * shrink for k in range(3, 6)]
        plastic = plastic + multiplier
    return components, plastic


def contact_column(contact_ref):
    rows = lax.broadcasted_iota(jnp.int32, (32, 16), 0)
    hit = jnp.where(contact_ref[...] == rows, 1.0, 0.0)
    return jnp.sum(hit, axis=1, keepdims=True)


def half_kernel(
    send_ref, link_ref, back_depth, back_strip, contact_ref, state_ref, own_acc, B_ref,
    m0, m1, m2, m3, sig_ref, plastic_ref, cohesion_ref, dens_ref,
    next_ref, n0, n1, n2, n3, S_ref, A_ref, src32, far32, acc,
):
    cross_terms(send_ref, link_ref, back_depth, back_strip, (m0, m1, m2, m3), B_ref, S_ref, A_ref, src32, far32, acc)
    flags = contact_column(contact_ref)
    own2 = own_acc.reshape(1024, 128)
    acc2 = acc.reshape(1024, 128)
    for c in range(4):
        at = slice(8 * c, 8 * c + 8)
        acceleration, strain = rates(state_ref, own2, acc2, flags[at], c)
        stress = [sig_ref[32 * k + 8 * c : 32 * k + 8 * c + 8, :] for k in range(6)]
        trial = elastic_step(stress, strain, 0.5)
        half_stress, _ = plastic_return(trial, plastic_ref[at, :], cohesion_ref[at, :])
        dens = dens_ref[at, :]
        square = dens * dens
        for k in range(3):
            x = slice(32 * k + 8 * c, 32 * k + 8 * c + 8)
            v = slice(96 + 32 * k + 8 * c, 96 + 32 * k + 8 * c + 8)
            motion = state_ref[v, :]
            next_ref[x, :] = state_ref[x, :] + 0.5 * time_step * motion
            next_ref[v, :] = motion + 0.5 * time_step * acceleration[k]
        for k in range(6):
            next_ref[192 + 32 * k + 8 * c : 200 + 32 * k + 8 * c, :] = half_stress[k] / square
    next_ref[384:512, :] = state_ref[384:512, :]
    gather_rims(send_ref, next_ref, (n0, n1, n2, n3))


def last_kernel(
    send_ref, link_ref, back_depth, back_strip, contact_ref, counts_ref, state_ref, own_acc, B_ref,
    m0, m1, m2, m3, sig_ref, plastic_ref, cohesion_ref, pos_ref, vel_ref,
    pos_out, vel_out, sig_out, plastic_out, S_ref, A_ref, src32, far32, acc,
):
    cross_terms(send_ref, link_ref, back_depth, back_strip, (m0, m1, m2, m3), B_ref, S_ref, A_ref, src32, far32, acc)
    flags = contact_column(contact_ref)
    column = lanes_to_column(counts_ref[...].astype(f32))
    lane = lax.broadcasted_iota(jnp.int32, (8, 128), 1).astype(f32)
    own2 = own_acc.reshape(1024, 128)
    acc2 = acc.reshape(1024, 128)
    for c in range(4):
        at = slice(8 * c, 8 * c + 8)
        keep = lane < column[at]
        acceleration, strain = rates(state_ref, own2, acc2, flags[at], c)
        stress = [sig_ref[32 * k + 8 * c : 32 * k + 8 * c + 8, :] for k in range(6)]
        trial = elastic_step(stress, strain, 1.0)
        new_stress, new_plastic = plastic_return(trial, plastic_ref[at, :], cohesion_ref[at, :])
        for k in range(3):
            x = slice(32 * k + 8 * c, 32 * k + 8 * c + 8)
            v = slice(96 + 32 * k + 8 * c, 96 + 32 * k + 8 * c + 8)
            pos_out[x, :] = jnp.where(keep, pos_ref[x, :] + time_step * state_ref[v, :], 0.0)
            vel_out[x, :] = jnp.where(keep, vel_ref[x, :] + time_step * acceleration[k], 0.0)
        for k in range(6):
            sig_out[32 * k + 8 * c : 32 * k + 8 * c + 8, :] = jnp.where(keep, new_stress[k], 0.0)
        plastic_out[at, :] = jnp.where(keep, new_plastic, 0.0)


SMEM = pl.BlockSpec(memory_space=pltpu.SMEM)
VMEM = pl.BlockSpec(memory_space=pltpu.VMEM)
params = pltpu.CompilerParams(vmem_limit_bytes=48 * 1024 * 1024)


def shape(*dims, dtype=f32):
    return jax.ShapeDtypeStruct(dims, dtype)


def tables(count):
    return [
        pltpu.VMEM((count, 64, 128), bf16),
        pltpu.VMEM((count, 128, 16), bf16),
        pltpu.VMEM((count * 32, 128), f32),
        pltpu.VMEM((count * 16, 128), f32),
    ]


def call(kernel, smem, vmem, outs, scratch):
    return pl.pallas_call(
        kernel,
        out_shape=outs,
        in_specs=[SMEM] * len(smem) + [VMEM] * len(vmem),
        out_specs=[VMEM] * len(outs),
        scratch_shapes=scratch,
        compiler_params=params,
    )(*smem, *vmem)


def shards(
    position, velocity, stress, plastic, particle_mass, density, cohesion,
    counts, block_pairs, pair_count, send_lists, cross_links, contact,
):
    pos = position.reshape(96, 128)
    vel = velocity.reshape(96, 128)
    sig = stress.reshape(192, 128)
    plastic_now = plastic.reshape(32, 128)
    mass = particle_mass.reshape(32, 128)
    dens = density.reshape(32, 128)
    cohesion_now = cohesion.reshape(32, 128)
    counts_now = counts.reshape(1, 32)
    pairs = block_pairs.reshape(128, 2)
    total = pair_count.reshape(1)
    send = send_lists.reshape(4, 16)
    links = cross_links.reshape(2, 48, 2)
    touched = contact.reshape(1, 16)

    back_depth = by_axis(links[0], "depth", 1, False)
    back_strip = by_axis(links[1], "strip", 1, True)
    rim = [shape(16 * ROWS, 128)] * 4
    state, *msgs = call(
        start_kernel, [send], [counts_now, pos, vel, sig, mass, dens], [shape(512, 128)] + rim, []
    )

    def swap(msgs):
        return (
            by_axis(msgs[1], "depth", -1, False),
            by_axis(msgs[0], "depth", 1, False),
            by_axis(msgs[3], "strip", -1, True),
            by_axis(msgs[2], "strip", 1, True),
        )

    def own(state):
        return call(
            own_kernel,
            [total, pairs],
            [state],
            [shape(32, 32, 128), shape(32, 16, 128, dtype=bf16)],
            tables(32) + [pltpu.VMEM((512, 128), f32), pltpu.VMEM((33, 32, 128), f32)],
        )

    cross_scratch = tables(64) + [pltpu.VMEM((32, 32, 128), f32)]
    far = swap(msgs)
    own_acc, to_side = own(state)
    state, *msgs = call(
        half_kernel,
        [send, links, back_depth, back_strip],
        [touched, state, own_acc, to_side, *far, sig, plastic_now, cohesion_now, dens],
        [shape(512, 128)] + rim,
        cross_scratch,
    )
    far = swap(msgs)
    own_acc, to_side = own(state)
    new_pos, new_vel, new_sig, new_plastic = call(
        last_kernel,
        [send, links, back_depth, back_strip],
        [touched, counts_now, state, own_acc, to_side, *far, sig, plastic_now, cohesion_now, pos, vel],
        [shape(96, 128), shape(96, 128), shape(192, 128), shape(32, 128)],
        cross_scratch,
    )
    return (
        new_pos.reshape(position.shape),
        new_vel.reshape(velocity.shape),
        new_sig.reshape(stress.shape),
        new_plastic.reshape(plastic.shape),
    )


def solution(mesh):
    def spec(rank):
        return P("strip", "depth", *([None] * (rank - 2)))

    return jax.shard_map(
        shards,
        mesh=mesh,
        in_specs=tuple(spec(r) for r in (5, 5, 5, 4, 4, 4, 4, 3, 4, 2, 4, 5, 3)),
        out_specs=tuple(spec(r) for r in (5, 5, 5, 4)),
        check_vma=False,
    )
```

time: 366 us -> 89.8 us (0.25)
  the two profiles are of different devices: /device:TPU:24 before, /device:TPU:17 now
where the time goes in v1:
time: 89.8 us; the launch traced here: 91.2 us
  Pallas kernels  50.6 us (56%)
  starting transfers between devices  24.8 us (28%)
  waiting for transfers between devices  8.6 us (10%)
  local copies, waits for them, and re-layouts  5.64 us (6%)
  between operations  1.56 us (2%)
    pallas_call x5, Pallas kernels, call(): pl.pallas_call(kernel, out_shape=outs, in_specs=[SMEM] * len(smem) + [VME...  50.6 us
    ppermute x10, starting transfers between devices, by_axis(): return lax.ppermute(value, axis, pairs)  24.8 us
    ppermute x10, waiting for transfers between devices, by_axis(): return lax.ppermute(value, axis, pairs)  8.6 us
    unnamed x34, local copies, waits for them, and re-layouts  5.45 us
  transfers between devices with their start and end apart: 10, of which 1 were waited for; matrix products, arithmetic and copies ran while one was open for 0% of the time, Pallas kernels for 24%

profile of v1, /device:TPU:17, one launch (start us, length us, event | category | flops | bytes accessed | tf_op | source)
XLA Modules:
  0.0 91.2 jit_solution(2420280150707270919)
XLA Ops:
  0.6 0.0 copy-start.10
  0.6 0.0 copy-start.13
  0.7 0.7 copy-done.10
  1.3 0.0 copy-done.13
  1.3 0.0 copy-start
  1.3 0.9 copy-done
  2.2 0.0 copy-start.2
  2.2 0.8 copy-done.2
  3.0 0.0 copy-start.4
  3.0 0.8 copy-done.4
  3.8 0.0 copy-start.6
  3.8 0.7 copy-done.6
  4.5 0.0 copy-start.11
  4.5 0.7 copy-done.11
  5.2 1.2 %shard_map.156 = (f32[512,128]{1,0:T(8,128)S(1)}, f32[256,128]{1,0:T(8,128)S(1)}, f32[256,128]{1,0:T(8,128)S(1)}, f32[256,128]{1,0:T(8,128)S(1)}, f32[256,128]{1,0:T(8,128)S(1)}) custom-call(s32[4,16]{1,0:T(4,128)S(1)} %bitcast.40, s32[1,32]{1,0:T(1,128)S(1)} %bitcast.46, f32[96,128]{1,0:T(8,128)S(1)} %bitcast.30, f32[96,128]{1,0:T(8,128)S(1)} %bitcast.32, ...), custom_call_target="tpu_custom_call" | custom-call | tf_op jit(solution)/shard_map/pallas_call | solution.py:372
  6.5 9.5 %collective-permute-start.2 = (f32[256,128]{1,0:T(8,128)S(1)}, f32[256,128]{1,0:T(8,128)S(1)}, u32[]{:S(2)}, u32[]{:S(2)}) collective-permute-start(f32[256,128]{1,0:T(8,128)S(1)} %get-tuple-element.25), channel_id=1, source_target_pairs={{1,0},{2,1},{3,2},{4,3},{5,4},{6,5},{7,6},{8,7},{9,8},{10,9},{11,1... | collective-permute-start | bytes 393224 | tf_op jit(solution)/shard_map/ppermute | solution.py:38
  15.9 0.0 copy-start.14
  15.9 1.9 %collective-permute-start.3 = (f32[256,128]{1,0:T(8,128)S(1)}, f32[256,128]{1,0:T(8,128)S(1)}, u32[]{:S(2)}, u32[]{:S(2)}) collective-permute-start(f32[256,128]{1,0:T(8,128)S(1)} %get-tuple-element.26), channel_id=1, source_target_pairs={{0,1},{1,2},{2,3},{3,4},{4,5},{5,6},{6,7},{7,8},{8,9},{9,10},{10,1... | collective-permute-start | bytes 393224 | tf_op jit(solution)/shard_map/ppermute | solution.py:38
  17.9 1.0 %collective-permute-start.4 = (f32[256,128]{1,0:T(8,128)S(1)}, f32[256,128]{1,0:T(8,128)S(1)}, u32[]{:S(2)}, u32[]{:S(2)}) collective-permute-start(f32[256,128]{1,0:T(8,128)S(1)} %get-tuple-element.27), channel_id=1, source_target_pairs={{0,192},{64,0},{128,64},{192,128},{1,193},{65,1},{129,65},{193,129... | collective-permute-start | bytes 393224 | tf_op jit(solution)/shard_map/ppermute | solution.py:38
  18.9 1.9 %collective-permute-start.5 = (f32[256,128]{1,0:T(8,128)S(1)}, f32[256,128]{1,0:T(8,128)S(1)}, u32[]{:S(2)}, u32[]{:S(2)}) collective-permute-start(f32[256,128]{1,0:T(8,128)S(1)} %get-tuple-element.28), channel_id=1, source_target_pairs={{0,64},{64,128},{128,192},{192,0},{1,65},{65,129},{129,193},{193,1... | collective-permute-start | bytes 393224 | tf_op jit(solution)/shard_map/ppermute | solution.py:38
  20.8 0.0 copy-done.14
  20.8 0.1 copy.18
  20.9 1.9 %collective-permute-start = (s32[48,2]{1,0:T(8,128)S(1)}, s32[48,2]{1,0:T(8,128)S(1)}, u32[]{:S(2)}, u32[]{:S(2)}) collective-permute-start(s32[48,2]{1,0:T(8,128)S(1)} %copy.18), channel_id=1, source_target_pairs={{0,1},{1,2},{2,3},{3,4},{4,5},{5,6},{6,7},{7,8},{8,9},{9,10},{10,1... | collective-permute-start | bytes 1160 | tf_op jit(solution)/shard_map/ppermute | solution.py:38
  22.8 0.1 copy.17
  22.9 0.1 copy.19
  23.0 0.0 copy-start.15
  23.0 8.6 %collective-permute-done.back_depth = s32[48,2]{1,0:T(8,128)S(1)} collective-permute-done((s32[48,2]{1,0:T(8,128)S(1)}, s32[48,2]{1,0:T(8,128)S(1)}, u32[]{:S(2)}, u32[]{:S(2)}) %collective-permute-start) | collective-permute-done | bytes 416 | tf_op jit(solution)/shard_map/ppermute | solution.py:38
  31.6 1.2 %collective-permute-start.1 = (s32[48,2]{1,0:T(8,128)S(1)}, s32[48,2]{1,0:T(8,128)S(1)}, u32[]{:S(2)}, u32[]{:S(2)}) collective-permute-start(s32[48,2]{1,0:T(8,128)S(1)} %copy.19), channel_id=1, source_target_pairs={{0,64},{64,128},{128,192},{192,0},{1,65},{65,129},{129,193},{193,1... | collective-permute-start | bytes 1160 | tf_op jit(solution)/shard_map/ppermute | solution.py:38
  33.4 0.0 copy-done.15
  33.5 0.1 copy.20
  33.6 0.0 copy-start.1
  33.6 0.0 copy-start.7
  33.6 0.0 copy-start.8
  33.6 0.0 copy-start.9
  33.6 10.9 %shard_map.157 = (f32[32,32,128]{2,1,0:T(8,128)S(1)}, bf16[32,16,128]{2,1,0:T(8,128)(2,1)S(1)}) custom-call(s32[1]{0:T(128)} %bitcast.21.count_ref, s32[128,2]{1,0:T(8,128)S(1)} %bitcast.26, f32[512,128]{1,0:T(8,128)S(1)} %get-tuple-element.22.state_ref), custom_call_target="tpu_custom_call" | custom-call | tf_op jit(solution)/shard_map/pallas_call | solution.py:372
  44.5 0.0 collective-permute-done.1.back_strip
  44.5 0.0 collective-permute-done.2.m0
  44.5 0.0 collective-permute-done.3.m1
  44.5 0.0 collective-permute-done.4.m2
  44.5 0.0 collective-permute-done.5.m3
  44.5 0.0 copy-start.12
  44.5 0.0 copy-done.1
  44.6 0.0 copy-done.7
  44.6 0.0 copy-done.8
  44.6 0.0 copy-done.9
  44.6 0.6 copy-done.12
  45.2 13.8 %shard_map.158 = (f32[512,128]{1,0:T(8,128)S(1)}, f32[256,128]{1,0:T(8,128)S(1)}, f32[256,128]{1,0:T(8,128)S(1)}, f32[256,128]{1,0:T(8,128)S(1)}, f32[256,128]{1,0:T(8,128)S(1)}) custom-call(s32[4,16]{1,0:T(4,128)S(1)} %bitcast.41, s32[2,48,2]{2,1,0:T(8,128)S(1)} %bitcast.28, s32[48,2]{1,0:T(8,128)S(1)} %collective-permute-done.back_depth, ...), custom_call_target="tpu_custom_call" | custom-call | tf_op jit(solution)/shard_map/pallas_call | solution.py:372
  59.0 3.6 %collective-permute-start.6 = (f32[256,128]{1,0:T(8,128)S(1)}, f32[256,128]{1,0:T(8,128)S(1)}, u32[]{:S(2)}, u32[]{:S(2)}) collective-permute-start(f32[256,128]{1,0:T(8,128)S(1)} %get-tuple-element.32), channel_id=1, source_target_pairs={{1,0},{2,1},{3,2},{4,3},{5,4},{6,5},{7,6},{8,7},{9,8},{10,9},{11,1... | collective-permute-start | bytes 393224 | tf_op jit(solution)/shard_map/ppermute | solution.py:38
  62.6 1.9 %collective-permute-start.7 = (f32[256,128]{1,0:T(8,128)S(1)}, f32[256,128]{1,0:T(8,128)S(1)}, u32[]{:S(2)}, u32[]{:S(2)}) collective-permute-start(f32[256,128]{1,0:T(8,128)S(1)} %get-tuple-element.33), channel_id=1, source_target_pairs={{0,1},{1,2},{2,3},{3,4},{4,5},{5,6},{6,7},{7,8},{8,9},{9,10},{10,1... | collective-permute-start | bytes 393224 | tf_op jit(solution)/shard_map/ppermute | solution.py:38
  64.5 0.1 collective-permute-start.8
  64.6 1.7 %collective-permute-start.9 = (f32[256,128]{1,0:T(8,128)S(1)}, f32[256,128]{1,0:T(8,128)S(1)}, u32[]{:S(2)}, u32[]{:S(2)}) collective-permute-start(f32[256,128]{1,0:T(8,128)S(1)} %get-tuple-element.35), channel_id=1, source_target_pairs={{0,64},{64,128},{128,192},{192,0},{1,65},{65,129},{129,193},{193,1... | collective-permute-start | bytes 393224 | tf_op jit(solution)/shard_map/ppermute | solution.py:38
  66.3 0.0 copy-start.3
  66.3 0.0 copy-start.5
  66.3 10.8 %shard_map.159 = (f32[32,32,128]{2,1,0:T(8,128)S(1)}, bf16[32,16,128]{2,1,0:T(8,128)(2,1)S(1)}) custom-call(s32[1]{0:T(128)} %bitcast.22.count_ref, s32[128,2]{1,0:T(8,128)S(1)} %bitcast.27, f32[512,128]{1,0:T(8,128)S(1)} %get-tuple-element.29.state_ref), custom_call_target="tpu_custom_call" | custom-call | tf_op jit(solution)/shard_map/pallas_call | solution.py:372
  77.2 0.0 collective-permute-done.6.m0
  77.2 0.0 collective-permute-done.7.m1
  77.2 0.0 collective-permute-done.8.m2
  77.2 0.0 collective-permute-done.9.m3
  77.2 0.0 copy-done.3
  77.2 0.0 copy-done.5
  77.2 14.0 %shard_map.160 = (f32[96,128]{1,0:T(8,128)}, f32[96,128]{1,0:T(8,128)}, f32[192,128]{1,0:T(8,128)}, f32[32,128]{1,0:T(8,128)}) custom-call(s32[4,16]{1,0:T(4,128)S(1)} %bitcast.42, s32[2,48,2]{2,1,0:T(8,128)S(1)} %bitcast.29, s32[48,2]{1,0:T(8,128)S(1)} %collective-permute-done.back_depth, s32[48,2]{1,0:T(8,128)S(1)} %collective-permute-done.1.back_strip, ...), custom_call_target="tpu_custom_call" | custom-call | tf_op jit(solution)/shard_map/pallas_call | solution.py:372
  (1 shorter events, 0.0 us)
Async XLA Ops:
  0.6 0.7 copy-start.10
  0.6 0.7 copy-start.13
  1.3 0.9 copy-start
  2.2 0.8 copy-start.2
  3.0 0.8 copy-start.4
  3.8 0.7 copy-start.6
  4.5 0.7 copy-start.11
  6.5 38.0 %collective-permute-start.2 = (f32[256,128]{1,0:T(8,128)S(1)}, f32[256,128]{1,0:T(8,128)S(1)}, u32[]{:S(2)}, u32[]{:S(2)}) collective-permute-start(f32[256,128]{1,0:T(8,128)S(1)} %get-tuple-element.25), channel_id=1, source_target_pairs={{1,0},{2,1},{3,2},{4,3},{5,4},{6,5},{7,6},{8,7},{9,8},{10,9},{11,1... | collective-permute-start | bytes 393224 | tf_op jit(solution)/shard_map/ppermute | solution.py:38
  15.9 4.9 %copy-start.14 = (s32[1,1,2,48,2]{3,4,2,1,0:T(2,128)S(1)}, s32[1,1,2,48,2]{3,4,2,1,0:T(2,128)}, u32[]{:S(2)}) copy-start(s32[1,1,2,48,2]{3,4,2,1,0:T(2,128)} %param.24) | copy-start | bytes 2308
  15.9 28.6 %collective-permute-start.3 = (f32[256,128]{1,0:T(8,128)S(1)}, f32[256,128]{1,0:T(8,128)S(1)}, u32[]{:S(2)}, u32[]{:S(2)}) collective-permute-start(f32[256,128]{1,0:T(8,128)S(1)} %get-tuple-element.26), channel_id=1, source_target_pairs={{0,1},{1,2},{2,3},{3,4},{4,5},{5,6},{6,7},{7,8},{8,9},{9,10},{10,1... | collective-permute-start | bytes 393224 | tf_op jit(solution)/shard_map/ppermute | solution.py:38
  17.9 26.7 %collective-permute-start.4 = (f32[256,128]{1,0:T(8,128)S(1)}, f32[256,128]{1,0:T(8,128)S(1)}, u32[]{:S(2)}, u32[]{:S(2)}) collective-permute-start(f32[256,128]{1,0:T(8,128)S(1)} %get-tuple-element.27), channel_id=1, source_target_pairs={{0,192},{64,0},{128,64},{192,128},{1,193},{65,1},{129,65},{193,129... | collective-permute-start | bytes 393224 | tf_op jit(solution)/shard_map/ppermute | solution.py:38
  18.9 25.6 %collective-permute-start.5 = (f32[256,128]{1,0:T(8,128)S(1)}, f32[256,128]{1,0:T(8,128)S(1)}, u32[]{:S(2)}, u32[]{:S(2)}) collective-permute-start(f32[256,128]{1,0:T(8,128)S(1)} %get-tuple-element.28), channel_id=1, source_target_pairs={{0,64},{64,128},{128,192},{192,0},{1,65},{65,129},{129,193},{193,1... | collective-permute-start | bytes 393224 | tf_op jit(solution)/shard_map/ppermute | solution.py:38
  20.9 10.7 %collective-permute-start = (s32[48,2]{1,0:T(8,128)S(1)}, s32[48,2]{1,0:T(8,128)S(1)}, u32[]{:S(2)}, u32[]{:S(2)}) collective-permute-start(s32[48,2]{1,0:T(8,128)S(1)} %copy.18), channel_id=1, source_target_pairs={{0,1},{1,2},{2,3},{3,4},{4,5},{5,6},{6,7},{7,8},{8,9},{9,10},{10,1... | collective-permute-start | bytes 1160 | tf_op jit(solution)/shard_map/ppermute | solution.py:38
  23.0 10.5 %copy-start.15 = (s32[1,1,128,2]{2,3,1,0:T(2,128)S(1)}, s32[1,1,128,2]{2,3,1,0:T(2,128)}, u32[]{:S(2)}) copy-start(s32[1,1,128,2]{2,3,1,0:T(2,128)} %param.21) | copy-start | bytes 3076
  31.6 12.9 %collective-permute-start.1 = (s32[48,2]{1,0:T(8,128)S(1)}, s32[48,2]{1,0:T(8,128)S(1)}, u32[]{:S(2)}, u32[]{:S(2)}) collective-permute-start(s32[48,2]{1,0:T(8,128)S(1)} %copy.19), channel_id=1, source_target_pairs={{0,64},{64,128},{128,192},{192,0},{1,65},{65,129},{129,193},{193,1... | collective-permute-start | bytes 1160 | tf_op jit(solution)/shard_map/ppermute | solution.py:38
  33.6 11.0 %copy-start.1 = (f32[1,1,6,32,128]{4,3,2,1,0:T(8,128)S(1)}, f32[1,1,6,32,128]{4,3,2,1,0:T(8,128)}, u32[]{:S(2)}) copy-start(f32[1,1,6,32,128]{4,3,2,1,0:T(8,128)} %param.15) | copy-start | bytes 294916
  33.6 11.0 %copy-start.7 = (f32[1,1,32,128]{3,2,1,0:T(8,128)S(1)}, f32[1,1,32,128]{3,2,1,0:T(8,128)}, u32[]{:S(2)}) copy-start(f32[1,1,32,128]{3,2,1,0:T(8,128)} %param.18) | copy-start | bytes 49156
  33.6 11.0 %copy-start.8 = (f32[1,1,32,128]{3,2,1,0:T(8,128)S(1)}, f32[1,1,32,128]{3,2,1,0:T(8,128)}, u32[]{:S(2)}) copy-start(f32[1,1,32,128]{3,2,1,0:T(8,128)} %param.16) | copy-start | bytes 49156
  33.6 11.0 %copy-start.9 = (f32[1,1,32,128]{3,2,1,0:T(8,128)S(1)}, f32[1,1,32,128]{3,2,1,0:T(8,128)}, u32[]{:S(2)}) copy-start(f32[1,1,32,128]{3,2,1,0:T(8,128)} %param.19) | copy-start | bytes 49156
  44.5 0.7 copy-start.12
  59.0 18.2 %collective-permute-start.6 = (f32[256,128]{1,0:T(8,128)S(1)}, f32[256,128]{1,0:T(8,128)S(1)}, u32[]{:S(2)}, u32[]{:S(2)}) collective-permute-start(f32[256,128]{1,0:T(8,128)S(1)} %get-tuple-element.32), channel_id=1, source_target_pairs={{1,0},{2,1},{3,2},{4,3},{5,4},{6,5},{7,6},{8,7},{9,8},{10,9},{11,1... | collective-permute-start | bytes 393224 | tf_op jit(solution)/shard_map/ppermute | solution.py:38
  62.6 14.6 %collective-permute-start.7 = (f32[256,128]{1,0:T(8,128)S(1)}, f32[256,128]{1,0:T(8,128)S(1)}, u32[]{:S(2)}, u32[]{:S(2)}) collective-permute-start(f32[256,128]{1,0:T(8,128)S(1)} %get-tuple-element.33), channel_id=1, source_target_pairs={{0,1},{1,2},{2,3},{3,4},{4,5},{5,6},{6,7},{7,8},{8,9},{9,10},{10,1... | collective-permute-start | bytes 393224 | tf_op jit(solution)/shard_map/ppermute | solution.py:38
  64.5 12.7 %collective-permute-start.8 = (f32[256,128]{1,0:T(8,128)S(1)}, f32[256,128]{1,0:T(8,128)S(1)}, u32[]{:S(2)}, u32[]{:S(2)}) collective-permute-start(f32[256,128]{1,0:T(8,128)S(1)} %get-tuple-element.34), channel_id=1, source_target_pairs={{0,192},{64,0},{128,64},{192,128},{1,193},{65,1},{129,65},{193,129... | collective-permute-start | bytes 393224 | tf_op jit(solution)/shard_map/ppermute | solution.py:38
  64.6 12.6 %collective-permute-start.9 = (f32[256,128]{1,0:T(8,128)S(1)}, f32[256,128]{1,0:T(8,128)S(1)}, u32[]{:S(2)}, u32[]{:S(2)}) collective-permute-start(f32[256,128]{1,0:T(8,128)S(1)} %get-tuple-element.35), channel_id=1, source_target_pairs={{0,64},{64,128},{128,192},{192,0},{1,65},{65,129},{129,193},{193,1... | collective-permute-start | bytes 393224 | tf_op jit(solution)/shard_map/ppermute | solution.py:38
  66.3 10.9 %copy-start.3 = (f32[1,1,3,32,128]{4,3,2,1,0:T(8,128)S(1)}, f32[1,1,3,32,128]{4,3,2,1,0:T(8,128)}, u32[]{:S(2)}) copy-start(f32[1,1,3,32,128]{4,3,2,1,0:T(8,128)} %param.13) | copy-start | bytes 147460
  66.3 10.9 %copy-start.5 = (f32[1,1,3,32,128]{4,3,2,1,0:T(8,128)S(1)}, f32[1,1,3,32,128]{4,3,2,1,0:T(8,128)}, u32[]{:S(2)}) copy-start(f32[1,1,3,32,128]{4,3,2,1,0:T(8,128)} %param.14) | copy-start | bytes 147460

commit v2 on v1

--- a/solution.py
+++ b/solution.py
@@ -9,7 +9,7 @@
 
 RETURN_ITERS = 4
 ROWS = 16
-GROUP = 16
+GROUP = 32
 
 smooth_len = 1.5
 kernel_coef = -105.0 / (3.141592653589793 * 1.5**5)
@@ -77,33 +77,40 @@
     return from_side, to_side
 
 
-def build_tables(row, base, count, src32, far32, S_ref, A_ref, to32, B_ref):
+def fill_rows(row, base, count, src32, far32, to32):
     for f, value in enumerate(source_rows(row)):
         src32[pl.ds(base * 32 + f, count, stride=32), :] = value
     from_side, to_side = distance_rows(row)
     for f, value in enumerate(from_side):
         far32[pl.ds(base * 16 + f, count, stride=16), :] = value
-    if B_ref is not None:
+    if to32 is not None:
         for f, value in enumerate(to_side):
             to32[pl.ds(base * 16 + f, count, stride=16), :] = value
 
 
-def finish_tables(total, src32, far32, S_ref, A_ref, to32, B_ref):
-    unroll = 4
-
-    def some(i, carry):
-        for u in range(unroll):
-            b = i * unroll + u
+def finish_tables(count, src32, far32, S_ref, A_ref):
+    def eight(i, carry):
+        flipped = far32[pl.ds(pl.multiple_of(i * 128, 128), 128), :].T
+        A_ref[i] = flipped.astype(bf16)
+        for u in range(8):
+            b = i * 8 + u
             value = src32[pl.ds(pl.multiple_of(b * 32, 32), 32), :]
             high = value.astype(bf16)
             S_ref[b, 0:32, :] = high
             S_ref[b, 32:64, :] = (value - high.astype(f32)).astype(bf16)
-            A_ref[b] = far32[pl.ds(pl.multiple_of(b * 16, 16), 16), :].T.astype(bf16)
-            if B_ref is not None:
-                B_ref[b] = to32[pl.ds(pl.multiple_of(b * 16, 16), 16), :].astype(bf16)
         return carry
 
-    lax.fori_loop(0, total // unroll, some, 0)
+    lax.fori_loop(0, count // 8, eight, 0)
+
+
+def pad_targets(B_ref, rows_of):
+    def one(b, carry):
+        B_ref[b, 0:112, :] = jnp.zeros((112, 128), bf16)
+        B_ref[b, 128:240, :] = jnp.zeros((112, 128), bf16)
+        B_ref[b, 112:128, :] = rows_of(b)
+        return carry
+
+    lax.fori_loop(0, 32, one, 0)
 
 
 def closeness_cubed(square):
@@ -117,7 +124,12 @@
         outs = []
         for u in range(GROUP):
             target, source = item(g, u)
-            square = jnp.dot(A_ref[source], B_ref[target[0]], preferred_element_type=f32)
+            start = pl.multiple_of(112 - 16 * lax.rem(source, 8), 16)
+            square = jnp.dot(
+                A_ref[lax.div(source, 8)],
+                B_ref[target[0], pl.ds(start, 128), :],
+                preferred_element_type=f32,
+            )
             kernel = closeness_cubed(square)
             high = kernel.astype(bf16)
             low = (kernel - high.astype(f32)).astype(bf16)
@@ -151,28 +163,58 @@
             ]
 
 
-def start_kernel(send_ref, counts_ref, pos_ref, vel_ref, sig_ref, mass_ref, dens_ref, state_ref, *msgs):
+def fetch(pairs, sem):
+    copies = [pltpu.make_async_copy(a, b, sem.at[i]) for i, (a, b) in enumerate(pairs)]
+    for copy in copies:
+        copy.start()
+    return copies
+
+
+def start_kernel(
+    send_hbm, counts_ref, links_ref, pos_hbm, vel_hbm, sig_hbm, mass_hbm, dens_hbm,
+    state_ref, m0, m1, m2, m3, send_ref, sig_ref, mass_ref, dens_ref, sem,
+):
+    copies = fetch(
+        [
+            (send_hbm, send_ref),
+            (pos_hbm, state_ref.at[0:96]),
+            (vel_hbm, state_ref.at[96:192]),
+            (sig_hbm, sig_ref),
+            (mass_hbm, mass_ref),
+            (dens_hbm, dens_ref),
+        ],
+        sem,
+    )
     column = lanes_to_column(counts_ref[...].astype(f32))
     lane = lax.broadcasted_iota(jnp.int32, (32, 128), 1).astype(f32)
+    for copy in copies:
+        copy.wait()
     mass = jnp.where(lane < column, mass_ref[...], 0.0)
     dens = dens_ref[...]
-    state_ref[0:96, :] = pos_ref[...]
-    state_ref[96:192, :] = vel_ref[...]
     square = dens * dens
     for k in range(6):
         state_ref[192 + 32 * k : 224 + 32 * k, :] = sig_ref[32 * k : 32 * k + 32, :] / square
     state_ref[384:416, :] = mass
     state_ref[416:448, :] = mass / dens
     state_ref[448:512, :] = jnp.zeros((64, 128), f32)
-    gather_rims(send_ref, state_ref, msgs)
-
-
-def own_kernel(count_ref, pairs_ref, state_ref, acc_ref, B_ref, S_ref, A_ref, src32, far32, to32, acc33):
+    gather_rims(send_ref, state_ref, (m0, m1, m2, m3))
+    m0[224:232, :] = links_ref[...]
+    m2[224:232, :] = links_ref[...]
+
+
+def own_kernel(count_ref, pairs_ref, state_ref, acc_ref, to_ref, S_ref, A_ref, B_ref, src32, far32, to32, acc33):
     def row(k):
         return state_ref[32 * k : 32 * k + 32, :]
 
-    build_tables(row, 0, 32, src32, far32, S_ref, A_ref, to32, B_ref)
-    finish_tables(32, src32, far32, S_ref, A_ref, to32, B_ref)
+    fill_rows(row, 0, 32, src32, far32, to32)
+    finish_tables(32, src32, far32, S_ref, A_ref)
+
+    def rows_of(b):
+        rows = to32[pl.ds(pl.multiple_of(b * 16, 16), 16), :].astype(bf16)
+        to_ref[b] = rows
+        return rows
+
+    pad_targets(B_ref, rows_of)
     acc33[...] = jnp.zeros_like(acc33)
     total = count_ref[0]
 
@@ -190,29 +232,31 @@
     acc_ref[...] = acc33[0:32]
 
 
-def cross_terms(send_ref, link_ref, back_depth, back_strip, msgs, B_ref, S_ref, A_ref, src32, far32, acc):
+def cross_terms(send_ref, link_ref, back_ref, msgs, to_ref, S_ref, A_ref, B_ref, src32, far32, acc, ready):
     for face in range(4):
         def row(k, face=face):
             return msgs[face][16 * k : 16 * k + 16, :]
 
-        build_tables(row, 16 * face, 16, src32, far32, S_ref, A_ref, None, None)
-    finish_tables(64, src32, far32, S_ref, A_ref, None, None)
+        fill_rows(row, 16 * face, 16, src32, far32, None)
+    finish_tables(64, src32, far32, S_ref, A_ref)
+    pad_targets(B_ref, lambda b: to_ref[b])
     acc[...] = jnp.zeros_like(acc)
+    ready()
 
     def item(g, u):
         q = g * (GROUP // 4) + u // 4
         if u % 4 == 0:
-            target = send_ref[0, link_ref[0, q, 0]]
-            source = link_ref[0, q, 1]
+            target = send_ref[0, link_ref[0, q]]
+            source = link_ref[1, q]
         elif u % 4 == 1:
-            target = send_ref[1, back_depth[q, 1]]
-            source = 16 + back_depth[q, 0]
+            target = send_ref[1, back_ref[1, q]]
+            source = 16 + back_ref[0, q]
         elif u % 4 == 2:
-            target = send_ref[2, link_ref[1, q, 0]]
-            source = 32 + link_ref[1, q, 1]
+            target = send_ref[2, link_ref[2, q]]
+            source = 32 + link_ref[3, q]
         else:
-            target = send_ref[3, back_strip[q, 1]]
-            source = 48 + back_strip[q, 0]
+            target = send_ref[3, back_ref[11, q]]
+            source = 48 + back_ref[10, q]
         return (target, target), source
 
     tile_loop(item, 48 // (GROUP // 4), S_ref, A_ref, B_ref, acc)
@@ -294,11 +338,17 @@
 
 
 def half_kernel(
-    send_ref, link_ref, back_depth, back_strip, contact_ref, state_ref, own_acc, B_ref,
+    send_ref, link_ref, contact_ref, state_ref, own_acc, to_ref,
     m0, m1, m2, m3, sig_ref, plastic_ref, cohesion_ref, dens_ref,
-    next_ref, n0, n1, n2, n3, S_ref, A_ref, src32, far32, acc,
+    next_ref, n0, n1, n2, n3, back_out, S_ref, A_ref, B_ref, src32, far32, acc, back_ref, sem,
 ):
-    cross_terms(send_ref, link_ref, back_depth, back_strip, (m0, m1, m2, m3), B_ref, S_ref, A_ref, src32, far32, acc)
+    back_out[0:8, :] = m1[224:232, :].astype(jnp.int32)
+    back_out[8:16, :] = m3[224:232, :].astype(jnp.int32)
+    copies = fetch([(back_out, back_ref)], sem)
+    cross_terms(
+        send_ref, link_ref, back_ref, (m0, m1, m2, m3), to_ref, S_ref, A_ref, B_ref, src32, far32, acc,
+        copies[0].wait,
+    )
     flags = contact_column(contact_ref)
     own2 = own_acc.reshape(1024, 128)
     acc2 = acc.reshape(1024, 128)
@@ -323,11 +373,14 @@
 
 
 def last_kernel(
-    send_ref, link_ref, back_depth, back_strip, contact_ref, counts_ref, state_ref, own_acc, B_ref,
+    send_ref, link_ref, back_ref, contact_ref, counts_ref, state_ref, own_acc, to_ref,
     m0, m1, m2, m3, sig_ref, plastic_ref, cohesion_ref, pos_ref, vel_ref,
-    pos_out, vel_out, sig_out, plastic_out, S_ref, A_ref, src32, far32, acc,
+    pos_out, vel_out, sig_out, plastic_out, S_ref, A_ref, B_ref, src32, far32, acc,
 ):
-    cross_terms(send_ref, link_ref, back_depth, back_strip, (m0, m1, m2, m3), B_ref, S_ref, A_ref, src32, far32, acc)
+    cross_terms(
+        send_ref, link_ref, back_ref, (m0, m1, m2, m3), to_ref, S_ref, A_ref, B_ref, src32, far32, acc,
+        lambda: None,
+    )
     flags = contact_column(contact_ref)
     column = lanes_to_column(counts_ref[...].astype(f32))
     lane = lax.broadcasted_iota(jnp.int32, (8, 128), 1).astype(f32)
@@ -352,6 +405,7 @@
 
 SMEM = pl.BlockSpec(memory_space=pltpu.SMEM)
 VMEM = pl.BlockSpec(memory_space=pltpu.VMEM)
+HBM = pl.BlockSpec(memory_space=pl.ANY)
 params = pltpu.CompilerParams(vmem_limit_bytes=48 * 1024 * 1024)
 
 
@@ -362,21 +416,22 @@
 def tables(count):
     return [
         pltpu.VMEM((count, 64, 128), bf16),
-        pltpu.VMEM((count, 128, 16), bf16),
+        pltpu.VMEM((count // 8, 128, 128), bf16),
+        pltpu.VMEM((32, 240, 128), bf16),
         pltpu.VMEM((count * 32, 128), f32),
         pltpu.VMEM((count * 16, 128), f32),
     ]
 
 
-def call(kernel, smem, vmem, outs, scratch):
+def call(kernel, smem, vmem, hbm, outs, scratch):
     return pl.pallas_call(
         kernel,
         out_shape=outs,
-        in_specs=[SMEM] * len(smem) + [VMEM] * len(vmem),
+        in_specs=[SMEM] * len(smem) + [VMEM] * len(vmem) + [HBM] * len(hbm),
         out_specs=[VMEM] * len(outs),
         scratch_shapes=scratch,
         compiler_params=params,
-    )(*smem, *vmem)
+    )(*smem, *vmem, *hbm)
 
 
 def shards(
@@ -394,15 +449,25 @@
     pairs = block_pairs.reshape(128, 2)
     total = pair_count.reshape(1)
     send = send_lists.reshape(4, 16)
-    links = cross_links.reshape(2, 48, 2)
+    links = jnp.swapaxes(cross_links.reshape(2, 48, 2), 1, 2).reshape(4, 48)
+    links_row = jnp.pad(links, ((0, 4), (0, 80))).astype(f32)
     touched = contact.reshape(1, 16)
 
-    back_depth = by_axis(links[0], "depth", 1, False)
-    back_strip = by_axis(links[1], "strip", 1, True)
     rim = [shape(16 * ROWS, 128)] * 4
-    state, *msgs = call(
-        start_kernel, [send], [counts_now, pos, vel, sig, mass, dens], [shape(512, 128)] + rim, []
-    )
+    state, *msgs = pl.pallas_call(
+        start_kernel,
+        out_shape=[shape(512, 128)] + rim,
+        in_specs=[HBM, VMEM, VMEM] + [HBM] * 5,
+        out_specs=[VMEM] * 5,
+        scratch_shapes=[
+            pltpu.SMEM((4, 16), jnp.int32),
+            pltpu.VMEM((192, 128), f32),
+            pltpu.VMEM((32, 128), f32),
+            pltpu.VMEM((32, 128), f32),
+            pltpu.SemaphoreType.DMA((6,)),
+        ],
+        compiler_params=params,
+    )(send, counts_now, links_row, pos, vel, sig, mass, dens)
 
     def swap(msgs):
         return (
@@ -417,6 +482,7 @@
             own_kernel,
             [total, pairs],
             [state],
+            [],
             [shape(32, 32, 128), shape(32, 16, 128, dtype=bf16)],
             tables(32) + [pltpu.VMEM((512, 128), f32), pltpu.VMEM((33, 32, 128), f32)],
         )
@@ -424,19 +490,21 @@
     cross_scratch = tables(64) + [pltpu.VMEM((32, 32, 128), f32)]
     far = swap(msgs)
     own_acc, to_side = own(state)
-    state, *msgs = call(
+    state, *msgs, back = call(
         half_kernel,
-        [send, links, back_depth, back_strip],
+        [send, links],
         [touched, state, own_acc, to_side, *far, sig, plastic_now, cohesion_now, dens],
-        [shape(512, 128)] + rim,
-        cross_scratch,
+        [],
+        [shape(512, 128)] + rim + [shape(16, 128, dtype=jnp.int32)],
+        cross_scratch + [pltpu.SMEM((16, 128), jnp.int32), pltpu.SemaphoreType.DMA((1,))],
     )
     far = swap(msgs)
     own_acc, to_side = own(state)
     new_pos, new_vel, new_sig, new_plastic = call(
         last_kernel,
-        [send, links, back_depth, back_strip],
+        [send, links, back],
         [touched, counts_now, state, own_acc, to_side, *far, sig, plastic_now, cohesion_now, pos, vel],
+        [],
         [shape(96, 128), shape(96, 128), shape(192, 128), shape(32, 128)],
         cross_scratch,
     )

time: 89.8 us -> 74.1 us (0.83)
  the two profiles are of different devices: /device:TPU:17 before, /device:TPU:16 now
where the time goes in v2:
time: 74.1 us; the launch traced here: 73.1 us
  Pallas kernels  41.6 us (56%)
  starting transfers between devices  24.4 us (33%)
  local copies, waits for them, and re-layouts  4.68 us (6%)
  between operations  1.5 us (2%)
    pallas_call x4, Pallas kernels, call(): pl.pallas_call(kernel, out_shape=outs, in_specs=[SMEM] * len(smem) + [VME...  40.4 us
    ppermute x8, starting transfers between devices, by_axis(): return lax.ppermute(value, axis, pairs)  24.4 us
    unnamed x31, local copies, waits for them, and re-layouts  4.68 us
  transfers between devices with their start and end apart: 8, of which 1 were waited for; matrix products, arithmetic and copies ran while one was open for 0% of the time, Pallas kernels for 26%

profile of v2, /device:TPU:16, one launch (start us, length us, event | category | flops | bytes accessed | tf_op | source)
XLA Modules:
  0.0 73.1 jit_solution(13721009827678376959)
XLA Ops:
  0.6 0.0 copy-start.8
  0.6 0.7 pad_convert_fusion.links_ref
  1.3 0.0 copy-start.9
  1.3 0.0 copy-start.13
  1.3 0.0 copy-done.8
  1.3 0.7 copy-done.9
  2.0 0.0 copy-done.13
  2.0 0.0 copy-start
  2.0 0.9 %copy-done = f32[1,1,6,32,128]{4,3,2,1,0:T(8,128)S(1)} copy-done((f32[1,1,6,32,128]{4,3,2,1,0:T(8,128)S(1)}, f32[1,1,6,32,128]{4,3,2,1,0:T(8,128)}, u32[]{:S(2)}) %copy-start) | copy-done | bytes 98328
  2.9 0.0 copy-start.2
  2.9 0.8 %copy-done.2 = f32[1,1,3,32,128]{4,3,2,1,0:T(8,128)S(1)} copy-done((f32[1,1,3,32,128]{4,3,2,1,0:T(8,128)S(1)}, f32[1,1,3,32,128]{4,3,2,1,0:T(8,128)}, u32[]{:S(2)}) %copy-start.2) | copy-done | bytes 49176
  3.7 0.0 copy-start.4
  3.7 0.8 %copy-done.4 = f32[1,1,3,32,128]{4,3,2,1,0:T(8,128)S(1)} copy-done((f32[1,1,3,32,128]{4,3,2,1,0:T(8,128)S(1)}, f32[1,1,3,32,128]{4,3,2,1,0:T(8,128)}, u32[]{:S(2)}) %copy-start.4) | copy-done | bytes 49176
  4.5 0.0 copy-start.11
  4.5 0.7 copy-done.11
  5.2 1.2 %shard_map.156 = (f32[512,128]{1,0:T(8,128)S(1)}, f32[256,128]{1,0:T(8,128)S(1)}, f32[256,128]{1,0:T(8,128)S(1)}, f32[256,128]{1,0:T(8,128)S(1)}, f32[256,128]{1,0:T(8,128)S(1)}) custom-call(s32[4,16]{1,0:T(4,128)S(1)} %bitcast.38, s32[1,32]{1,0:T(1,128)S(1)} %bitcast.47, f32[8,128]{1,0:T(8,128)S(1)} %pad_convert_fusion.links_ref, f32[96,128]{1,0:T(8,128)S(1)} %bitcast.28, ...), custom_call_target="tpu_custom_call" | custom-call | tf_op jit(solution)/shard_map/pallas_call | solution.py:457
  6.4 9.7 %collective-permute-start = (f32[256,128]{1,0:T(8,128)S(1)}, f32[256,128]{1,0:T(8,128)S(1)}, u32[]{:S(2)}, u32[]{:S(2)}) collective-permute-start(f32[256,128]{1,0:T(8,128)S(1)} %get-tuple-element.26), channel_id=1, source_target_pairs={{1,0},{2,1},{3,2},{4,3},{5,4},{6,5},{7,6},{8,7},{9,8},{10,9},{11,1... | collective-permute-start | bytes 393224 | tf_op jit(solution)/shard_map/ppermute | solution.py:38
  16.2 1.9 %collective-permute-start.1 = (f32[256,128]{1,0:T(8,128)S(1)}, f32[256,128]{1,0:T(8,128)S(1)}, u32[]{:S(2)}, u32[]{:S(2)}) collective-permute-start(f32[256,128]{1,0:T(8,128)S(1)} %get-tuple-element.27), channel_id=1, source_target_pairs={{0,1},{1,2},{2,3},{3,4},{4,5},{5,6},{6,7},{7,8},{8,9},{9,10},{10,1... | collective-permute-start | bytes 393224 | tf_op jit(solution)/shard_map/ppermute | solution.py:38
  18.1 1.4 %collective-permute-start.2 = (f32[256,128]{1,0:T(8,128)S(1)}, f32[256,128]{1,0:T(8,128)S(1)}, u32[]{:S(2)}, u32[]{:S(2)}) collective-permute-start(f32[256,128]{1,0:T(8,128)S(1)} %get-tuple-element.28), channel_id=1, source_target_pairs={{0,192},{64,0},{128,64},{192,128},{1,193},{65,1},{129,65},{193,129... | collective-permute-start | bytes 393224 | tf_op jit(solution)/shard_map/ppermute | solution.py:38
  19.5 0.0 copy-start.14
  19.5 0.0 collective-permute-start.3
  20.2 0.0 copy-done.14
  20.2 0.1 copy.17
  20.3 0.0 copy-start.1
  20.3 0.0 copy-start.6
  20.3 0.0 copy-start.7
  20.3 9.5 %shard_map.157 = (f32[32,32,128]{2,1,0:T(8,128)S(1)}, bf16[32,16,128]{2,1,0:T(8,128)(2,1)S(1)}) custom-call(s32[1]{0:T(128)} %bitcast.21.count_ref, s32[128,2]{1,0:T(8,128)S(1)} %bitcast.26, f32[512,128]{1,0:T(8,128)S(1)} %get-tuple-element.23.state_ref), custom_call_target="tpu_custom_call" | custom-call | tf_op jit(solution)/shard_map/pallas_call | solution.py:427
  29.9 0.0 collective-permute-done.m0
  29.9 0.0 collective-permute-done.1.m1
  29.9 0.0 collective-permute-done.2.m2
  29.9 0.0 collective-permute-done.3.m3
  29.9 0.0 copy-start.10
  29.9 0.0 copy-start.12
  30.0 0.0 copy-done.1
  30.0 0.0 copy-done.6
  30.0 0.0 copy-done.7
  30.0 0.6 copy-done.10
  30.6 0.0 copy-done.12
  30.6 10.4 %shard_map.158 = (f32[512,128]{1,0:T(8,128)S(1)}, f32[256,128]{1,0:T(8,128)S(1)}, f32[256,128]{1,0:T(8,128)S(1)}, f32[256,128]{1,0:T(8,128)S(1)}, f32[256,128]{1,0:T(8,128)S(1)}, /*index=5*/s32[16,128]{1,0:T(8,128)S(1)}) custom-call(s32[4,16]{1,0:T(4,128)S(1)} %bitcast.39, s32[4,48]{1,0:T(4,128)S(1)} %bitcast.42, s32[1,16]{1,0:T(1,128)S(1)} %bitcast.45, ...), custom_call_target="tpu_custom_call" | custom-call | tf_op jit(solution)/shard_map/pallas_call | solution.py:427
  41.0 8.8 %collective-permute-start.4 = (f32[256,128]{1,0:T(8,128)S(1)}, f32[256,128]{1,0:T(8,128)S(1)}, u32[]{:S(2)}, u32[]{:S(2)}) collective-permute-start(f32[256,128]{1,0:T(8,128)S(1)} %get-tuple-element.34), channel_id=1, source_target_pairs={{1,0},{2,1},{3,2},{4,3},{5,4},{6,5},{7,6},{8,7},{9,8},{10,9},{11,1... | collective-permute-start | bytes 393224 | tf_op jit(solution)/shard_map/ppermute | solution.py:38
  49.8 1.9 %collective-permute-start.5 = (f32[256,128]{1,0:T(8,128)S(1)}, f32[256,128]{1,0:T(8,128)S(1)}, u32[]{:S(2)}, u32[]{:S(2)}) collective-permute-start(f32[256,128]{1,0:T(8,128)S(1)} %get-tuple-element.35), channel_id=1, source_target_pairs={{0,1},{1,2},{2,3},{3,4},{4,5},{5,6},{6,7},{7,8},{8,9},{9,10},{10,1... | collective-permute-start | bytes 393224 | tf_op jit(solution)/shard_map/ppermute | solution.py:38
  51.8 0.1 collective-permute-start.6
  51.9 0.5 collective-permute-start.7
  52.4 0.0 copy-start.3
  52.4 0.0 copy-start.5
  52.4 9.7 %shard_map.159 = (f32[32,32,128]{2,1,0:T(8,128)S(1)}, bf16[32,16,128]{2,1,0:T(8,128)(2,1)S(1)}) custom-call(s32[1]{0:T(128)} %bitcast.22.count_ref, s32[128,2]{1,0:T(8,128)S(1)} %bitcast.27, f32[512,128]{1,0:T(8,128)S(1)} %get-tuple-element.31.state_ref), custom_call_target="tpu_custom_call" | custom-call | tf_op jit(solution)/shard_map/pallas_call | solution.py:427
  62.1 0.0 collective-permute-done.4.m0
  62.1 0.3 collective-permute-done.5.m1
  62.4 0.0 collective-permute-done.6.m2
  62.4 0.0 collective-permute-done.7.m3
  62.4 0.0 copy-done.3
  62.4 0.0 copy-done.5
  62.4 10.7 %shard_map.160 = (f32[96,128]{1,0:T(8,128)}, f32[96,128]{1,0:T(8,128)}, f32[192,128]{1,0:T(8,128)}, f32[32,128]{1,0:T(8,128)}) custom-call(s32[4,16]{1,0:T(4,128)S(1)} %bitcast.40, s32[4,48]{1,0:T(4,128)S(1)} %bitcast.43, s32[16,128]{1,0:T(8,128)S(1)} %get-tuple-element.30.back_ref, s32[1,16]{1,0:T(1,128)S(1)} %bitcast.46, s32[1,32]{1,0:T(1,128)S(1)} %bitcast.48, ...), custom_call_target="tpu_custom_call" | custom-call | tf_op jit(solution)/shard_map/pallas_call | solution.py:427
Async XLA Ops:
  0.6 0.7 copy-start.8
  1.3 0.7 copy-start.9
  1.3 0.7 copy-start.13
  2.0 0.9 %copy-start = (f32[1,1,6,32,128]{4,3,2,1,0:T(8,128)S(1)}, f32[1,1,6,32,128]{4,3,2,1,0:T(8,128)}, u32[]{:S(2)}) copy-start(f32[1,1,6,32,128]{4,3,2,1,0:T(8,128)} %param.15) | copy-start | bytes 294916
  2.9 0.8 %copy-start.2 = (f32[1,1,3,32,128]{4,3,2,1,0:T(8,128)S(1)}, f32[1,1,3,32,128]{4,3,2,1,0:T(8,128)}, u32[]{:S(2)}) copy-start(f32[1,1,3,32,128]{4,3,2,1,0:T(8,128)} %param.13) | copy-start | bytes 147460
  3.7 0.8 %copy-start.4 = (f32[1,1,3,32,128]{4,3,2,1,0:T(8,128)S(1)}, f32[1,1,3,32,128]{4,3,2,1,0:T(8,128)}, u32[]{:S(2)}) copy-start(f32[1,1,3,32,128]{4,3,2,1,0:T(8,128)} %param.14) | copy-start | bytes 147460
  4.5 0.7 copy-start.11
  6.4 23.5 %collective-permute-start = (f32[256,128]{1,0:T(8,128)S(1)}, f32[256,128]{1,0:T(8,128)S(1)}, u32[]{:S(2)}, u32[]{:S(2)}) collective-permute-start(f32[256,128]{1,0:T(8,128)S(1)} %get-tuple-element.26), channel_id=1, source_target_pairs={{1,0},{2,1},{3,2},{4,3},{5,4},{6,5},{7,6},{8,7},{9,8},{10,9},{11,1... | collective-permute-start | bytes 393224 | tf_op jit(solution)/shard_map/ppermute | solution.py:38
  16.2 13.7 %collective-permute-start.1 = (f32[256,128]{1,0:T(8,128)S(1)}, f32[256,128]{1,0:T(8,128)S(1)}, u32[]{:S(2)}, u32[]{:S(2)}) collective-permute-start(f32[256,128]{1,0:T(8,128)S(1)} %get-tuple-element.27), channel_id=1, source_target_pairs={{0,1},{1,2},{2,3},{3,4},{4,5},{5,6},{6,7},{7,8},{8,9},{9,10},{10,1... | collective-permute-start | bytes 393224 | tf_op jit(solution)/shard_map/ppermute | solution.py:38
  18.1 11.8 %collective-permute-start.2 = (f32[256,128]{1,0:T(8,128)S(1)}, f32[256,128]{1,0:T(8,128)S(1)}, u32[]{:S(2)}, u32[]{:S(2)}) collective-permute-start(f32[256,128]{1,0:T(8,128)S(1)} %get-tuple-element.28), channel_id=1, source_target_pairs={{0,192},{64,0},{128,64},{192,128},{1,193},{65,1},{129,65},{193,129... | collective-permute-start | bytes 393224 | tf_op jit(solution)/shard_map/ppermute | solution.py:38
  19.5 0.7 copy-start.14
  19.5 10.4 %collective-permute-start.3 = (f32[256,128]{1,0:T(8,128)S(1)}, f32[256,128]{1,0:T(8,128)S(1)}, u32[]{:S(2)}, u32[]{:S(2)}) collective-permute-start(f32[256,128]{1,0:T(8,128)S(1)} %get-tuple-element.29), channel_id=1, source_target_pairs={{0,64},{64,128},{128,192},{192,0},{1,65},{65,129},{129,193},{193,1... | collective-permute-start | bytes 393224 | tf_op jit(solution)/shard_map/ppermute | solution.py:38
  20.3 9.7 %copy-start.1 = (f32[1,1,6,32,128]{4,3,2,1,0:T(8,128)S(1)}, f32[1,1,6,32,128]{4,3,2,1,0:T(8,128)}, u32[]{:S(2)}) copy-start(f32[1,1,6,32,128]{4,3,2,1,0:T(8,128)} %param.15) | copy-start | bytes 294916
  20.3 9.7 %copy-start.6 = (f32[1,1,32,128]{3,2,1,0:T(8,128)S(1)}, f32[1,1,32,128]{3,2,1,0:T(8,128)}, u32[]{:S(2)}) copy-start(f32[1,1,32,128]{3,2,1,0:T(8,128)} %param.16) | copy-start | bytes 49156
  20.3 9.7 %copy-start.7 = (f32[1,1,32,128]{3,2,1,0:T(8,128)S(1)}, f32[1,1,32,128]{3,2,1,0:T(8,128)}, u32[]{:S(2)}) copy-start(f32[1,1,32,128]{3,2,1,0:T(8,128)} %param.19) | copy-start | bytes 49156
  29.9 0.7 copy-start.10
  29.9 0.7 copy-start.12
  41.0 21.0 %collective-permute-start.4 = (f32[256,128]{1,0:T(8,128)S(1)}, f32[256,128]{1,0:T(8,128)S(1)}, u32[]{:S(2)}, u32[]{:S(2)}) collective-permute-start(f32[256,128]{1,0:T(8,128)S(1)} %get-tuple-element.34), channel_id=1, source_target_pairs={{1,0},{2,1},{3,2},{4,3},{5,4},{6,5},{7,6},{8,7},{9,8},{10,9},{11,1... | collective-permute-start | bytes 393224 | tf_op jit(solution)/shard_map/ppermute | solution.py:38
  49.8 12.6 %collective-permute-start.5 = (f32[256,128]{1,0:T(8,128)S(1)}, f32[256,128]{1,0:T(8,128)S(1)}, u32[]{:S(2)}, u32[]{:S(2)}) collective-permute-start(f32[256,128]{1,0:T(8,128)S(1)} %get-tuple-element.35), channel_id=1, source_target_pairs={{0,1},{1,2},{2,3},{3,4},{4,5},{5,6},{6,7},{7,8},{8,9},{9,10},{10,1... | collective-permute-start | bytes 393224 | tf_op jit(solution)/shard_map/ppermute | solution.py:38
  51.8 10.7 %collective-permute-start.6 = (f32[256,128]{1,0:T(8,128)S(1)}, f32[256,128]{1,0:T(8,128)S(1)}, u32[]{:S(2)}, u32[]{:S(2)}) collective-permute-start(f32[256,128]{1,0:T(8,128)S(1)} %get-tuple-element.36), channel_id=1, source_target_pairs={{0,192},{64,0},{128,64},{192,128},{1,193},{65,1},{129,65},{193,129... | collective-permute-start | bytes 393224 | tf_op jit(solution)/shard_map/ppermute | solution.py:38
  51.9 10.6 %collective-permute-start.7 = (f32[256,128]{1,0:T(8,128)S(1)}, f32[256,128]{1,0:T(8,128)S(1)}, u32[]{:S(2)}, u32[]{:S(2)}) collective-permute-start(f32[256,128]{1,0:T(8,128)S(1)} %get-tuple-element.37), channel_id=1, source_target_pairs={{0,64},{64,128},{128,192},{192,0},{1,65},{65,129},{129,193},{193,1... | collective-permute-start | bytes 393224 | tf_op jit(solution)/shard_map/ppermute | solution.py:38
  52.4 10.1 %copy-start.3 = (f32[1,1,3,32,128]{4,3,2,1,0:T(8,128)S(1)}, f32[1,1,3,32,128]{4,3,2,1,0:T(8,128)}, u32[]{:S(2)}) copy-start(f32[1,1,3,32,128]{4,3,2,1,0:T(8,128)} %param.13) | copy-start | bytes 147460
  52.4 10.1 %copy-start.5 = (f32[1,1,3,32,128]{4,3,2,1,0:T(8,128)S(1)}, f32[1,1,3,32,128]{4,3,2,1,0:T(8,128)}, u32[]{:S(2)}) copy-start(f32[1,1,3,32,128]{4,3,2,1,0:T(8,128)} %param.14) | copy-start | bytes 147460
